TPU v7x, 128 devices: a whole 4x4x4 slice. The times are simulated.
128 devices in a mesh: col: 16 (over x, y_hi, core), row: 8 (over z, y_lo).
Axes of the slice: x: 4, y: 4 (y_hi: 2, y_lo: 2; y = y_hi * 2 + y_lo), z: 4, core: 2. Of those that a mesh axis runs over, the one named last changes fastest.
Arguments:
- matrix: float32 [28672, 8192], P('row', 'col'), may hold values from -6 to 6
- vectors: float32 [8192, 8192], P('row', 'col'), may hold values from -6 to 6
Outputs:
- next_matrix: float32 [28672, 8192], P('row', 'col')
- next_vectors: float32 [8192, 8192], P('row', 'col')
All inputs are finite; a program needn't handle non-finite values.
Results may differ from a plain program's by a relative error of at most 0.0003.
Values sent between devices are 32-bit elements; how exact they have to be, the bound alone decides.
No kernel may reach another device: no remote copies, remote signals or barrier semaphores. Data moves between devices by JAX's collectives and lax.ppermute only.
A program may use at most 128 MiB of HBM per device.

v0:
```python
import jax
import jax.numpy as jnp
from jax import lax
from jax.sharding import PartitionSpec as P

POLAR_STEPS = 10


def from_behind(block, axis, distance):
    devices = range(lax.axis_size(axis))
    route = [(i - distance, i) for i in devices if i - distance in devices]
    return lax.ppermute(block, axis, route)


def product(left, right):
    return jnp.dot(left, right, precision=lax.Precision.HIGHEST, preferred_element_type=jnp.float32)


def make_transform(gram):
    lower = jnp.linalg.cholesky(gram)
    ident = jnp.eye(gram.shape[0], dtype=gram.dtype)
    inverse = jax.scipy.linalg.solve_triangular(lower, ident, lower=True)
    start = inverse.T * jnp.diagonal(lower)[None, :]
    magnitude = jnp.abs(start)
    spectral_bound = jnp.sqrt(
        jnp.max(jnp.sum(magnitude, axis=0)) * jnp.max(jnp.sum(magnitude, axis=1))
    )
    approx = start / spectral_bound
    for step in range(POLAR_STEPS):
        square = product(approx.T, approx)
        approx = 1.5 * approx - 0.5 * product(approx, square)
    return approx


def on_device(matrix, vectors):
    width_pair = matrix.shape[1]
    half_cols = width_pair // 2
    count_col = lax.axis_size("col")
    own_index = lax.axis_index("col")
    at_first = own_index == 0
    at_last = own_index == count_col - 1
    partial_gram = lax.dot_general(
        matrix,
        matrix,
        (((0,), (0,)), ((), ())),
        precision=lax.Precision.HIGHEST,
        preferred_element_type=jnp.float32,
    )
    gram_total = lax.psum(partial_gram, "row")
    transform = make_transform(gram_total)
    moved = product(matrix, transform)
    turned = product(vectors, transform)
    moved_top = moved[:, :half_cols]
    moved_bottom = moved[:, half_cols:]
    turned_top = turned[:, :half_cols]
    turned_bottom = turned[:, half_cols:]
    upward_matrix = jnp.where(at_first, moved_bottom, moved_top)
    upward_vectors = jnp.where(at_first, turned_bottom, turned_top)
    from_left = from_behind((upward_matrix, upward_vectors), "col", 1)
    from_right = from_behind((moved_bottom, turned_bottom), "col", -1)
    new_top_matrix = jnp.where(at_first, moved_top, from_left[0])
    new_top_vectors = jnp.where(at_first, turned_top, from_left[1])
    new_bottom_matrix = jnp.where(at_last, moved_top, from_right[0])
    new_bottom_vectors = jnp.where(at_last, turned_top, from_right[1])
    next_matrix = jnp.concatenate([new_top_matrix, new_bottom_matrix], axis=1)
    next_vectors = jnp.concatenate([new_top_vectors, new_bottom_vectors], axis=1)
    return (next_matrix, next_vectors)


def solution(mesh):
    in_specs = (P("row", "col"), P("row", "col"))
    out_specs = (P("row", "col"), P("row", "col"))
    return jax.shard_map(
        on_device, mesh=mesh, in_specs=in_specs, out_specs=out_specs, check_vma=False
    )
```

profile of v0, /device:TPU:3, one launch (start us, length us, event | category | flops | bytes accessed | tf_op | source)
XLA Modules:
  0.0 490.7 jit_solution(5931823373027047892)
XLA Ops:
  7.2 18.4 %fusion.44 = f32[512,512]{0,1:T(8,128)} fusion(f32[3584,512]{1,0:T(8,128)} %param.2), kind=kOutput, calls=%fused_computation.106 | convolution fusion | flops 11274289152 | bytes 8388608 | tf_op jit(solution)/shard_map/dot_general | solution.py:42
  27.6 77.1 %all-reduce.3.cloned.1.call-done = f32[512,512]{0,1:T(8,128)} async-done(((f32[512,512]{0,1:T(8,128)}), f32[512,512]{0,1:T(8,128)}) %all-reduce.3.cloned.1.call-update) | async-done | bytes 1048592 | tf_op jit(solution)/shard_map/psum | solution.py:49
  108.7 11.7 %cholesky.104 = f32[128,128]{1,0:T(8,128)S(1)} custom-call(f32[128,128]{1,0:T(8,128)S(1)} %cholesky.266), custom_call_target="Cholesky" | custom-call | tf_op jit(solution)/shard_map/jit(cholesky)/cholesky | solution.py:20
  120.6 9.8 %custom-call.31 = f32[1,128,128]{1,2,0:T(8,128)S(1)} custom-call(f32[1,128,128]{2,1,0:T(8,128)S(1)} %get-tuple-element.45), custom_call_target="InvertDiagBlocksLowerTriangular" | custom-call | tf_op jit(solution)/shard_map/jit(cholesky)/cholesky | solution.py:20
  132.9 11.7 %cholesky.217 = f32[128,128]{1,0:T(8,128)S(1)} custom-call(f32[128,128]{1,0:T(8,128)S(1)} %cholesky.270), custom_call_target="Cholesky" | custom-call | tf_op jit(solution)/shard_map/jit(cholesky)/cholesky | solution.py:20
  144.7 10.0 %custom-call.32 = f32[1,128,128]{1,2,0:T(8,128)S(1)} custom-call(f32[1,128,128]{2,1,0:T(8,128)S(1)} %get-tuple-element.42), custom_call_target="InvertDiagBlocksLowerTriangular" | custom-call | tf_op jit(solution)/shard_map/jit(cholesky)/cholesky | solution.py:20
  156.2 11.7 %cholesky.238 = f32[128,128]{1,0:T(8,128)S(1)} custom-call(f32[128,128]{1,0:T(8,128)S(1)} %cholesky.275), custom_call_target="Cholesky" | custom-call | tf_op jit(solution)/shard_map/jit(cholesky)/cholesky | solution.py:20
  168.0 9.8 %custom-call.33 = f32[1,128,128]{1,2,0:T(8,128)S(1)} custom-call(f32[1,128,128]{2,1,0:T(8,128)S(1)} %get-tuple-element.39), custom_call_target="InvertDiagBlocksLowerTriangular" | custom-call | tf_op jit(solution)/shard_map/jit(cholesky)/cholesky | solution.py:20
  179.2 11.7 %cholesky.255 = f32[128,128]{1,0:T(8,128)S(1)} custom-call(f32[128,128]{1,0:T(8,128)S(1)} %convolution_subtract_fusion.5), custom_call_target="Cholesky" | custom-call | tf_op jit(solution)/shard_map/jit(cholesky)/cholesky | solution.py:20
  198.4 14.1 %while.1 = (s32[]{:T(128)}, f32[512,512]{1,0:T(8,128)}, s32[4,2]{0,1:T(2,128)S(1)}, f32[4,128,128]{2,1,0:T(8,128)}, s32[]{:T(128)}) while((s32[]{:T(128)}, f32[512,512]{1,0:T(8,128)}, s32[4,2]{0,1:T(2,128)S(1)}, f32[4,128,128]{2,1,0:T(8,128)}, s32[]{:T(128)}) %tuple.39), condition=%wide.while_cond, body=%wide.while_body.sunk | while | flops 2 | bytes 132205 | solution.py:22
  206.2 2.9 bitcast_dynamic-update-slice_fusion.2
  212.5 40.7 %custom-call.34 = f32[4,128,128]{1,2,0:T(8,128)} custom-call(f32[4,128,128]{2,1,0:T(8,128)} %get-tuple-element.9), custom_call_target="InvertDiagBlocksLowerTriangular" | custom-call | tf_op jit(solution)/shard_map/jit(_solve_triangular)/triangular_solve | solution.py:22
  269.7 4.5 gather_fusion
  278.4 3.4 fusion.20
  318.3 23.6 %convolution_bitcast_fusion = f32[3584,512]{0,1:T(8,128)S(1)} fusion(f32[512,512]{1,0:T(8,128)S(1)} %fusion, f32[3584,512]{1,0:T(8,128)S(1)} %bitcast.99), kind=kOutput, calls=%fused_computation.4 | convolution fusion | flops 11274289152 | bytes 15728640 | tf_op jit(solution)/shard_map/dot_general | solution.py:16
  341.8 3.8 slice_select_fusion.2
  347.1 9.3 %collective-permute-start = (f32[3584,256]{0,1:T(8,128)}, f32[3584,256]{0,1:T(8,128)}, u32[]{:S(2)}, u32[]{:S(2)}) collective-permute-start(f32[3584,256]{0,1:T(8,128)} %get-tuple-element.30), channel_id=1, source_target_pairs={{0,8},{8,16},{16,24},{24,32},{32,40},{40,48},{48,56},{56,64},{64,7... | collective-permute-start | bytes 11010056 | tf_op jit(solution)/shard_map/ppermute | solution.py:12
  358.3 6.7 %convolution_bitcast_fusion.1 = f32[1024,512]{0,1:T(8,128)S(1)} fusion(f32[512,512]{1,0:T(8,128)S(1)} %fusion, f32[1024,512]{1,0:T(8,128)S(1)} %copy-done), kind=kOutput, calls=%fused_computation.9 | convolution fusion | flops 3221225472 | bytes 5242880 | tf_op jit(solution)/shard_map/dot_general | solution.py:16
  367.6 5.1 %collective-permute-start.2 = (f32[1024,256]{0,1:T(8,128)}, f32[1024,256]{0,1:T(8,128)}, u32[]{:S(2)}, u32[]{:S(2)}) collective-permute-start(f32[1024,256]{0,1:T(8,128)} %get-tuple-element.34), channel_id=1, source_target_pairs={{0,8},{8,16},{16,24},{24,32},{32,40},{40,48},{48,56},{56,64},{64,7... | collective-permute-start | bytes 3145736 | tf_op jit(solution)/shard_map/ppermute | solution.py:12
  374.6 83.7 %collective-permute-done.2 = f32[1024,256]{0,1:T(8,128)} collective-permute-done((f32[1024,256]{0,1:T(8,128)}, f32[1024,256]{0,1:T(8,128)}, u32[]{:S(2)}, u32[]{:S(2)}) %collective-permute-start.2) | collective-permute-done | bytes 1048608 | tf_op jit(solution)/shard_map/ppermute | solution.py:12
  463.8 2.9 copy.21
  466.7 5.1 %slice_select_fusion.1 = (f32[3584,256]{0,1:T(8,128)S(1)}, f32[3584,256]{0,1:T(8,128)S(1)}) fusion(f32[3584,256]{0,1:T(8,128)} %collective-permute-done, f32[3584,512]{0,1:T(8,128)} %copy-done.1, pred[]{:T(512)S(6)} %eq.15, f32[3584,256]{0,1:T(8,128)} %collective-permute-done.1, pred[]{:T(512)S(6)} %eq.17), kind=kLoop, calls=%fused_computation.6 | loop fusion | flops 1835008 | bytes 18350082 | tf_op jit(solution)/shard_map/jit(_where)/select_n | solution.py:61
  471.8 3.4 pad_maximum_fusion
  475.3 8.4 %copy.20 = f32[3584,512]{1,0:T(8,128)} copy(f32[3584,512]{0,1:T(8,128)} %pad_maximum_fusion) | data formatting | bytes 14680064
  (106 shorter events, 96.5 us)
Async XLA Ops:
  7.2 351.2 %copy-start = (f32[1024,512]{1,0:T(8,128)S(1)}, f32[1024,512]{1,0:T(8,128)}, u32[]{:S(2)}) copy-start(f32[1024,512]{1,0:T(8,128)} %param.3) | copy-start | bytes 6291460
  7.2 97.5 %all-reduce.3.cloned.1.call-start = ((), (), s32[]{:S(2)}) async-start(), calls=%async_computation | async-start | bytes 2097152 | tf_op jit(solution)/shard_map/psum | solution.py:49
  107.7 1.0 copy-start.5
  191.0 5.1 %copy-start.3 = (f32[512,512]{1,0:T(8,128)}, f32[512,512]{1,0:T(8,128)S(1)}, u32[]{:S(2)}) copy-start(f32[512,512]{1,0:T(8,128)S(1)} %get-tuple-element.37) | copy-start | bytes 3145732
  257.1 2.8 copy-start.4
  259.9 0.7 copy-start.6
  267.4 11.0 %copy-start.7 = (f32[128,512]{0,1:T(8,128)S(1)}, f32[128,512]{0,1:T(8,128)}, u32[]{:S(2)}) copy-start(f32[128,512]{0,1:T(8,128)} %copy.17) | copy-start | bytes 786436
  274.2 7.6 %copy-start.8 = (f32[128,512]{0,1:T(8,128)S(1)}, f32[128,512]{0,1:T(8,128)}, u32[]{:S(2)}) copy-start(f32[128,512]{0,1:T(8,128)} %copy.16) | copy-start | bytes 786436
  274.2 7.6 %copy-start.9 = (f32[128,512]{0,1:T(8,128)S(1)}, f32[128,512]{0,1:T(8,128)}, u32[]{:S(2)}) copy-start(f32[128,512]{0,1:T(8,128)} %copy.15) | copy-start | bytes 786436
  274.3 7.6 %copy-start.10 = (f32[128,512]{0,1:T(8,128)S(1)}, f32[128,512]{0,1:T(8,128)}, u32[]{:S(2)}) copy-start(f32[128,512]{0,1:T(8,128)} %fusion.32) | copy-start | bytes 786436
  308.5 9.8 %slice-start = ((s8[7340032]{0:T(1024)(128)(4,1)}), s8[4194304]{0:T(1024)(128)(4,1)S(1)}, s32[]{:S(2)}) async-start(s8[7340032]{0:T(1024)(128)(4,1)} %bitcast.98), calls=%async_computation.1 | async-start | bytes 8388608
  312.2 6.0 %slice-start.1 = ((s8[7340032]{0:T(1024)(128)(4,1)}), s8[3145728]{0:T(1024)(128)(4,1)S(1)}, s32[]{:S(2)}) async-start(s8[7340032]{0:T(1024)(128)(4,1)} %bitcast.98), calls=%async_computation.2 | async-start | bytes 6291456
  341.8 5.3 %copy-start.1 = (f32[3584,512]{0,1:T(8,128)}, f32[3584,512]{0,1:T(8,128)S(1)}, u32[]{:S(2)}) copy-start(f32[3584,512]{0,1:T(8,128)S(1)} %convolution_bitcast_fusion) | copy-start | bytes 22020100
  347.1 119.6 %collective-permute-start = (f32[3584,256]{0,1:T(8,128)}, f32[3584,256]{0,1:T(8,128)}, u32[]{:S(2)}, u32[]{:S(2)}) collective-permute-start(f32[3584,256]{0,1:T(8,128)} %get-tuple-element.30), channel_id=1, source_target_pairs={{0,8},{8,16},{16,24},{24,32},{32,40},{40,48},{48,56},{56,64},{64,7... | collective-permute-start | bytes 11010056 | tf_op jit(solution)/shard_map/ppermute | solution.py:12
  356.4 110.3 %collective-permute-start.1 = (f32[3584,256]{0,1:T(8,128)}, f32[3584,256]{0,1:T(8,128)}, u32[]{:S(2)}, u32[]{:S(2)}) collective-permute-start(f32[3584,256]{0,1:T(8,128)} %get-tuple-element.31), channel_id=1, source_target_pairs={{8,0},{16,8},{24,16},{32,24},{40,32},{48,40},{56,48},{64,56},{72,6... | collective-permute-start | bytes 11010056 | tf_op jit(solution)/shard_map/ppermute | solution.py:12
  365.1 1.3 copy-start.2
  367.6 90.7 %collective-permute-start.2 = (f32[1024,256]{0,1:T(8,128)}, f32[1024,256]{0,1:T(8,128)}, u32[]{:S(2)}, u32[]{:S(2)}) collective-permute-start(f32[1024,256]{0,1:T(8,128)} %get-tuple-element.34), channel_id=1, source_target_pairs={{0,8},{8,16},{16,24},{24,32},{32,40},{40,48},{48,56},{56,64},{64,7... | collective-permute-start | bytes 3145736 | tf_op jit(solution)/shard_map/ppermute | solution.py:12
  372.7 87.5 %collective-permute-start.3 = (f32[1024,256]{0,1:T(8,128)S(1)}, f32[1024,256]{0,1:T(8,128)}, u32[]{:S(2)}, u32[]{:S(2)}) collective-permute-start(f32[1024,256]{0,1:T(8,128)S(1)} %get-tuple-element.35), channel_id=1, source_target_pairs={{8,0},{16,8},{24,16},{32,24},{40,32},{48,40},{56,48},{64,56},{72,6... | collective-permute-start | bytes 3145736 | tf_op jit(solution)/shard_map/ppermute | solution.py:12
Sparse Core Ops, SparseCore 0:
  25.8 78.8 all-reduce.2
where the time goes:
time: 497 us; the launch traced here: 491 us
  waiting for transfers between devices  163 us (33%)
  other arithmetic  146 us (29%)
  matrix products  105 us (21%)
  local copies, waits for them, and re-layouts  40.4 us (8%)
  between operations  18.7 us (4%)
  starting transfers between devices  18.3 us (4%)
    ppermute x4, waiting for transfers between devices, from_behind(): return lax.ppermute(block, axis, route)  85.5 us
    another operation x14, other arithmetic, make_transform(): lower = jnp.linalg.cholesky(gram)  79.1 us
    psum x1, waiting for transfers between devices, on_device(): gram_total = lax.psum(partial_gram, 'row')  77.1 us
    dot_general x22, matrix products, product(): jnp.dot(left, right, precision=lax.Precision.HIGHEST, preferred_element_t...  69.9 us
    another operation x3, other arithmetic, make_transform(): inverse = jax.scipy.linalg.solve_triangular(lower, ident, lower=True)  43.1 us
    dot_general x1, matrix products, on_device(): lax.dot_general(matrix, matrix, (((0,), (0,)), ((), ())), precision=lax.P...  18.4 us
    ppermute x4, starting transfers between devices, from_behind(): return lax.ppermute(block, axis, route)  18.3 us
    unnamed x28, local copies, waits for them, and re-layouts  15.7 us
  transfers between devices with their start and end apart: 5, of which 3 were waited for; matrix products, arithmetic and copies ran while one was open for 3% of the time, Pallas kernels for 0%

commit v1 on v0

v1 whole, which is shorter than its diff:
```python
import functools

import jax
import jax.numpy as jnp
from jax import lax
from jax.experimental import pallas as pl
from jax.experimental.pallas import tpu as pltpu
from jax.sharding import PartitionSpec as P

POLAR_STEPS = 10
LEAF = 128
F32 = jnp.float32
BF16 = jnp.bfloat16
NT = (((1,), (1,)), ((), ()))
NN = (((1,), (0,)), ((), ()))
TN = (((0,), (0,)), ((), ()))


def split(x):
    hi = x.astype(BF16)
    return hi, (x - hi.astype(F32)).astype(BF16)


def dot3(a, b, dims=NN):
    dot = functools.partial(lax.dot_general, dimension_numbers=dims, preferred_element_type=F32)
    return dot(a[0], b[1]) + dot(a[1], b[0]) + dot(a[0], b[0])


def dot_high(a, b, dims=NN):
    return lax.dot_general(a, b, dims, precision=lax.Precision.HIGHEST, preferred_element_type=F32)


def eliminate_leaf(block):
    groups = LEAF // 8
    rows = [block[8 * g : 8 * g + 8, :] for g in range(groups)]
    inv_pivot = []
    lane = lax.broadcasted_iota(jnp.int32, (8, LEAF), 1)
    sub = lax.broadcasted_iota(jnp.int32, (8, LEAF), 0)
    for p in range(groups):
        j0 = 8 * p
        panel = rows[p]
        cols = [jnp.broadcast_to(panel[:, j0 + u : j0 + u + 1], (8, LEAF)) for u in range(8)]
        s = [[None] * 8 for _ in range(8)]
        for t in range(8):
            for u in range(t, 8):
                s[t][u] = jnp.broadcast_to(cols[u][t : t + 1, :], (8, LEAF))
        in_panel = (lane >= j0) & (lane < j0 + 8)
        unit = (lane - j0 == sub).astype(F32)
        panel = jnp.where(in_panel, unit, panel)
        line = [jnp.broadcast_to(panel[t : t + 1, :], (8, LEAF)) for t in range(8)]
        recip = []
        for t in range(8):
            r = 1.0 / s[t][t]
            recip.append(r)
            for u in range(t + 1, 8):
                f = s[t][u] * r
                for v in range(u, 8):
                    s[u][v] = s[u][v] - f * s[t][v]
                line[u] = line[u] - f * line[t]
        done = line[7]
        inv = recip[7]
        for t in range(6, -1, -1):
            done = jnp.where(sub == t, line[t], done)
            inv = jnp.where(sub == t, recip[t], inv)
        rows[p] = done
        inv_pivot.append(inv)
        for g in range(p + 1, groups):
            cur = rows[g]
            left = [jnp.broadcast_to(cur[:, j0 + u : j0 + u + 1], (8, LEAF)) for u in range(8)]
            cur = jnp.where(in_panel, 0.0, cur)
            for t in range(8):
                m = left[t] * recip[t]
                for u in range(t + 1, 8):
                    left[u] = left[u] - m * s[t][u]
                cur = cur - m * line[t]
            rows[g] = cur
    return jnp.concatenate(rows, axis=0), jnp.concatenate(inv_pivot, axis=0)


def gram_kernel(x_ref, out_ref, same, cross):
    step = pl.program_id(0)
    half = x_ref.shape[1] // 2

    @pl.when(step == 0)
    def _():
        same[...] = jnp.zeros_like(same)
        cross[...] = jnp.zeros_like(cross)

    hi, lo = split(x_ref[...])
    dot = functools.partial(lax.dot_general, dimension_numbers=TN, preferred_element_type=F32)
    same[:half, :] += dot(hi[:, :half], hi)
    same[half:, half:] += dot(hi[:, half:], hi[:, half:])
    cross[...] += dot(hi, lo)

    @pl.when(step == pl.num_programs(0) - 1)
    def _():
        out_ref[:half] = same[:half, :half] + (cross[:half, :half] + cross[:half, :half].T)
        out_ref[half : 2 * half] = same[:half, half:] + (cross[:half, half:] + cross[half:, :half].T)
        out_ref[2 * half :] = same[half:, half:] + (cross[half:, half:] + cross[half:, half:].T)


def make_gram(x, tile=512):
    rows, n = x.shape
    half = n // 2
    return pl.pallas_call(
        gram_kernel,
        grid=(rows // tile,),
        out_shape=jax.ShapeDtypeStruct((3 * half, half), F32),
        in_specs=[pl.BlockSpec((tile, n), lambda i: (i, 0))],
        out_specs=pl.BlockSpec((3 * half, half), lambda i: (0, 0)),
        scratch_shapes=[pltpu.VMEM((n, n), F32), pltpu.VMEM((n, n), F32)],
        compiler_params=pltpu.CompilerParams(vmem_limit_bytes=32 * 2**20),
    )(x)


def sum_over_rows(gram):
    count = lax.axis_size("row")
    pieces = gram.reshape(count, gram.shape[0] // count, gram.shape[1])
    theirs = lax.all_to_all(pieces, "row", 0, 0, tiled=True)
    own = jnp.sum(theirs, axis=0)
    spread = jnp.broadcast_to(own[None], pieces.shape)
    return lax.all_to_all(spread, "row", 0, 0, tiled=True).reshape(gram.shape)


def transform_kernel(swap_ref, gram_ref, hi_ref, lo_ref, work):
    n = work.shape[0]
    half = n // 2
    work[:half, :half] = gram_ref[:half]
    work[:half, half:] = gram_ref[half : 2 * half]
    work[half:, :half] = gram_ref[half : 2 * half].T
    work[half:, half:] = gram_ref[2 * half :]

    def block_step(p, carry):
        at = pl.ds(pl.multiple_of(p * LEAF, LEAF), LEAF)
        block, inv = eliminate_leaf(work[at, at])
        r = lax.broadcasted_iota(jnp.int32, (LEAF, LEAF), 0)
        c = lax.broadcasted_iota(jnp.int32, (LEAF, LEAF), 1)
        lower = jnp.where(c <= r, block, 0.0)
        work[at, at] = (r == c).astype(F32)
        panel = dot_high(lower, work[at, :])
        col = lax.broadcasted_iota(jnp.int32, (LEAF, n), 1)
        scaled = jnp.where(col >= (p + 1) * LEAF, panel * inv[:, :1], 0.0)
        work[at, :] = panel
        later = lax.broadcasted_iota(jnp.int32, (n, LEAF), 0) >= (p + 1) * LEAF
        work[:, at] = jnp.where(later, 0.0, work[:, at])
        work[...] -= dot_high(scaled, panel, TN)
        return carry

    lax.fori_loop(0, n // LEAF, block_step, 0)
    r = lax.broadcasted_iota(jnp.int32, (n, n), 0)
    c = lax.broadcasted_iota(jnp.int32, (n, n), 1)
    start = jnp.where(c <= r, work[...], 0.0)
    mag = jnp.abs(start)
    bound = jnp.sqrt(jnp.max(jnp.sum(mag, axis=0, keepdims=True)) * jnp.max(jnp.sum(mag, axis=1, keepdims=True)))
    work[...] = start / bound

    def polar_step(k, carry):
        z = work[...]
        zs = split(z)
        g = dot3(zs, zs, NT)
        work[...] = 1.5 * z - 0.5 * dot3(split(g), zs)
        return carry

    lax.fori_loop(0, POLAR_STEPS, polar_step, 0)
    for side in range(2):
        begin = pl.multiple_of(jnp.bitwise_xor(swap_ref[0], side) * half, half)
        hi, lo = split(work[pl.ds(begin, half), :].T)
        hi_ref[:, side * half : (side + 1) * half] = hi
        lo_ref[:, side * half : (side + 1) * half] = lo


def make_transform(gram, swap):
    n = 2 * gram.shape[1]
    return pl.pallas_call(
        transform_kernel,
        out_shape=[jax.ShapeDtypeStruct((n, n), BF16)] * 2,
        in_specs=[pl.BlockSpec(memory_space=pltpu.SMEM), pl.BlockSpec(memory_space=pltpu.VMEM)],
        out_specs=[pl.BlockSpec(memory_space=pltpu.VMEM)] * 2,
        scratch_shapes=[pltpu.VMEM((n, n), F32)],
        compiler_params=pltpu.CompilerParams(vmem_limit_bytes=48 * 2**20),
    )(swap, gram)


def apply_kernel(x_ref, hi_ref, lo_ref, up_ref, down_ref):
    half = up_ref.shape[1]
    xs = split(x_ref[...])
    both = dot3(xs, (hi_ref[...], lo_ref[...]))
    up_ref[...] = both[:, :half]
    down_ref[...] = both[:, half:]


def apply_rows(x, begin, rows, parts, tile=512):
    n = x.shape[1]
    half = n // 2
    first = begin // tile
    return pl.pallas_call(
        apply_kernel,
        grid=(rows // tile,),
        out_shape=[jax.ShapeDtypeStruct((rows, half), F32)] * 2,
        in_specs=[
            pl.BlockSpec((tile, n), lambda i: (first + i, 0)),
            pl.BlockSpec((n, n), lambda i: (0, 0)),
            pl.BlockSpec((n, n), lambda i: (0, 0)),
        ],
        out_specs=[pl.BlockSpec((tile, half), lambda i: (i, 0))] * 2,
        compiler_params=pltpu.CompilerParams(vmem_limit_bytes=32 * 2**20),
        cost_estimate=pl.CostEstimate(flops=6 * rows * n * n, bytes_accessed=8 * rows * n, transcendentals=0),
    )(x, *parts)


def place_kernel(begin, ends_ref, from_left, from_right, own_up, own_down, *rest):
    out, sems = rest[-2], rest[-1]
    rows, half = from_left.shape
    at = pl.ds(begin, rows)
    for side, (own, other) in enumerate(((own_down, from_left), (own_up, from_right))):
        target = out.at[at, pl.ds(side * half, half)]

        @pl.when(ends_ref[side] == 1)
        def _():
            pltpu.make_async_copy(own, target, sems.at[side]).start()

        @pl.when(ends_ref[side] == 0)
        def _():
            pltpu.make_async_copy(other, target, sems.at[side]).start()

    for side in range(2):
        target = out.at[at, pl.ds(side * half, half)]
        pltpu.make_async_copy(from_left, target, sems.at[side]).wait()


def place_rows(out, shape, begin, ends, blocks):
    args = [ends, *blocks] + ([] if out is None else [out])
    return pl.pallas_call(
        functools.partial(place_kernel, begin),
        out_shape=jax.ShapeDtypeStruct(shape, F32),
        in_specs=[pl.BlockSpec(memory_space=pltpu.SMEM)] + [pl.BlockSpec(memory_space=pl.ANY)] * (len(args) - 1),
        out_specs=pl.BlockSpec(memory_space=pl.ANY),
        scratch_shapes=[pltpu.SemaphoreType.DMA((2,))],
        input_output_aliases={} if out is None else {len(args) - 1: 0},
    )(*args)


CHUNKS = ((0, 0, 512), (0, 512, 1024), (0, 1536, 1024), (1, 0, 1024), (0, 2560, 1024))


def on_device(matrix, vectors):
    count_col = lax.axis_size("col")
    own_index = lax.axis_index("col")
    ends = jnp.stack([own_index == 0, own_index == count_col - 1]).astype(jnp.int32)
    upward = [(i, i + 1) for i in range(count_col - 1)]
    downward = [(i + 1, i) for i in range(count_col - 1)]
    sources = (matrix, vectors)
    results = [None, None]
    gram = sum_over_rows(make_gram(matrix))
    parts = make_transform(gram, ends)
    for which, begin, rows in CHUNKS:
        up, down = apply_rows(sources[which], begin, rows, parts)
        from_left = lax.ppermute(up, "col", upward)
        from_right = lax.ppermute(down, "col", downward)
        results[which] = place_rows(
            results[which], sources[which].shape, begin, ends, (from_left, from_right, up, down)
        )
    return tuple(results)


def solution(mesh):
    in_specs = (P("row", "col"), P("row", "col"))
    out_specs = (P("row", "col"), P("row", "col"))
    return jax.shard_map(
        on_device, mesh=mesh, in_specs=in_specs, out_specs=out_specs, check_vma=False
    )
```

time: 497 us -> 476 us (0.958)
  Pallas kernels: 0 us -> 356 us
  other arithmetic: 146 us -> 1.26 us
  waiting for transfers between devices: 163 us -> 47.7 us
  matrix products: 105 us -> 0 us
  local copies, waits for them, and re-layouts: 40.4 us -> 11.1 us
  starting transfers between devices: 18.3 us -> 39.1 us
  blocking collectives: 0 us -> 18.3 us
  between operations: 18.7 us -> 1.05 us
    pallas_call x0 -> x12, Pallas kernels: none -> 356 us  [the longest x5 295 us: place_rows(): pl.pallas_call(functools.partial(place_kernel, begin), out_shape=jax.Shap...]
    another operation x17 -> x0, other arithmetic: 122 us -> none  [the longest x14 79.1 us: make_transform(): lower = jnp.linalg.cholesky(gram)]
    dot_general x23 -> x0, matrix products: 88.3 us -> none  [the longest x22 69.9 us: product(): jnp.dot(left, right, precision=lax.Precision.HIGHEST, preferred_element_t...]
    psum x1 -> x0, waiting for transfers between devices: 77.1 us -> none  [on_device(): gram_total = lax.psum(partial_gram, 'row')]
    ppermute x4 -> x10, waiting for transfers between devices: 85.5 us -> 36.6 us  [the longest x5 36.6 us: on_device(): from_left = lax.ppermute(up, 'col', upward)]
    another operation x20 -> x0, local copies, waits for them, and re-layouts: 18.6 us -> none
    all_to_all x0 -> x1, blocking collectives: none -> 18.3 us  [sum_over_rows(): theirs = lax.all_to_all(pieces, 'row', 0, 0, tiled=True)]
    another operation x13 -> x0, matrix products: 16.8 us -> none  [the longest x7 11.3 us: make_transform(): inverse = jax.scipy.linalg.solve_triangular(lower, ident, lower=True)]
  transfers between devices with their start and end apart: 5 -> 11, of which waited for: 3 -> 2; matrix products, arithmetic and copies ran while one was open for 3% -> 0% of each run, Pallas kernels for 0% -> 50%
where the time goes in v1:
time: 476 us; the launch traced here: 475 us
  Pallas kernels  356 us (75%)
  waiting for transfers between devices  47.7 us (10%)
  starting transfers between devices  39.1 us (8%)
  blocking collectives  18.3 us (4%)
  local copies, waits for them, and re-layouts  11.1 us (2%)
    pallas_call x5, Pallas kernels, place_rows(): pl.pallas_call(functools.partial(place_kernel, begin), out_shape=jax.Shap...  295 us
    pallas_call x1, Pallas kernels, make_transform(): pl.pallas_call(transform_kernel, out_shape=[jax.ShapeDtypeStruct((n, n),...  44.2 us
    ppermute x5, waiting for transfers between devices, on_device(): from_left = lax.ppermute(up, 'col', upward)  36.6 us
    ppermute x5, starting transfers between devices, on_device(): from_left = lax.ppermute(up, 'col', upward)  24.8 us
    all_to_all x1, blocking collectives, sum_over_rows(): theirs = lax.all_to_all(pieces, 'row', 0, 0, tiled=True)  18.3 us
    pallas_call x5, Pallas kernels, apply_rows(): pl.pallas_call(apply_kernel, grid=(rows // tile,), out_shape=[jax.ShapeDt...  11.8 us
    all_to_all x1, waiting for transfers between devices, sum_over_rows(): return lax.all_to_all(spread, 'row', 0, 0, tiled=True).reshape(gram.shape)  11.1 us
    unnamed x38, local copies, waits for them, and re-layouts  10.2 us
  transfers between devices with their start and end apart: 11, of which 2 were waited for; matrix products, arithmetic and copies ran while one was open for 0% of the time, Pallas kernels for 50%

profile of v1, /device:TPU:3, one launch (start us, length us, event | category | flops | bytes accessed | tf_op | source)
XLA Modules:
  0.0 474.6 jit_solution(18194845868575204417)
XLA Ops:
  0.6 3.1 copy-done
  3.7 5.3 %shard_map.41 = f32[768,256]{1,0:T(8,128)S(1)} custom-call(f32[3584,512]{1,0:T(8,128)S(1)} %copy-done), custom_call_target="tpu_custom_call" | custom-call | tf_op jit(solution)/shard_map/pallas_call | solution.py:105
  9.1 18.3 %all_to_all.10 = f32[8,96,256]{2,1,0:T(8,128)} all-to-all(f32[8,96,256]{2,1,0:T(8,128)S(1)} %bitcast.6), channel_id=1, replica_groups=mesh['col'=16,'row'=8] {'row'}, dimensions={0} | all-to-all | bytes 1572864 | tf_op jit(solution)/shard_map/all_to_all | solution.py:119
  29.5 4.2 all-to-all-start.1
  33.8 11.1 %all-to-all-done.1 = f32[8,96,256]{2,1,0:T(8,128)} async-done(((f32[8,96,256]{2,1,0:T(8,128)}), f32[8,96,256]{2,1,0:T(8,128)}, u32[]{:S(2)}, u32[]{:S(2)}) %all-to-all-start.1) | async-done | bytes 786464 | tf_op jit(solution)/shard_map/all_to_all | solution.py:122
  44.9 44.2 %shard_map.42 = (bf16[512,512]{1,0:T(8,128)(2,1)S(1)}, bf16[512,512]{1,0:T(8,128)(2,1)S(1)}) custom-call(s32[2]{0:T(128)S(1)} %add_convert_fusion.swap_ref.ends_ref, f32[768,256]{1,0:T(8,128)} %bitcast.3.gram_ref), custom_call_target="tpu_custom_call" | custom-call | tf_op jit(solution)/shard_map/pallas_call | solution.py:174
  89.0 3.1 copy-done.1
  92.2 2.8 shard_map.45
  94.9 7.2 %collective-permute-start.4 = (f32[1024,256]{1,0:T(8,128)S(1)}, f32[1024,256]{1,0:T(8,128)S(1)}, u32[]{:S(2)}, u32[]{:S(2)}) collective-permute-start(f32[1024,256]{1,0:T(8,128)S(1)} %get-tuple-element.20.own_up), channel_id=1, source_target_pairs={{0,8},{8,16},{16,24},{24,32},{32,40},{40,48},{48,56},{56,64},{64,7... | collective-permute-start | bytes 3145736 | tf_op jit(solution)/shard_map/ppermute | solution.py:258
  102.1 2.0 shard_map.51
  104.1 1.9 collective-permute-start.8
  106.1 2.4 collective-permute-start.9
  109.5 4.7 collective-permute-start.6
  116.1 3.0 shard_map.44
  119.2 3.0 shard_map.43
  122.2 36.6 %collective-permute-done.6.from_left = f32[512,256]{1,0:T(8,128)S(1)} collective-permute-done((f32[512,256]{1,0:T(8,128)S(1)}, f32[512,256]{1,0:T(8,128)S(1)}, u32[]{:S(2)}, u32[]{:S(2)}) %collective-permute-start.6) | collective-permute-done | bytes 524320 | tf_op jit(solution)/shard_map/ppermute | solution.py:258
  160.7 5.9 %collective-permute-start.2 = (f32[1024,256]{1,0:T(8,128)}, f32[1024,256]{1,0:T(8,128)S(1)}, u32[]{:S(2)}, u32[]{:S(2)}) collective-permute-start(f32[1024,256]{1,0:T(8,128)} %get-tuple-element.18.own_up), channel_id=1, source_target_pairs={{0,8},{8,16},{16,24},{24,32},{32,40},{40,48},{48,56},{56,64},{64,7... | collective-permute-start | bytes 3145736 | tf_op jit(solution)/shard_map/ppermute | solution.py:258
  166.6 1.9 collective-permute-start.3
  168.6 5.1 %collective-permute-start = (f32[1024,256]{1,0:T(8,128)}, f32[1024,256]{1,0:T(8,128)S(1)}, u32[]{:S(2)}, u32[]{:S(2)}) collective-permute-start(f32[1024,256]{1,0:T(8,128)} %get-tuple-element.16.own_up), channel_id=1, source_target_pairs={{0,8},{8,16},{16,24},{24,32},{32,40},{40,48},{48,56},{56,64},{64,7... | collective-permute-start | bytes 3145736 | tf_op jit(solution)/shard_map/ppermute | solution.py:258
  176.7 33.6 %shard_map.47.rest_0_ = f32[3584,512]{1,0:T(8,128)} custom-call(s32[2]{0:T(128)} %copy-done.7, f32[512,256]{1,0:T(8,128)} %copy-done.15, f32[512,256]{1,0:T(8,128)} %copy-done.16, f32[512,256]{1,0:T(8,128)} %copy-done.5, f32[512,256]{1,0:T(8,128)} %copy-done.6), custom_call_target="tpu_custom_call" | custom-call | tf_op jit(solution)/shard_map/pallas_call | solution.py:233
  210.2 65.3 %shard_map.52 = f32[1024,512]{1,0:T(8,128)} custom-call(s32[2]{0:T(128)} %copy-done.7, f32[1024,256]{1,0:T(8,128)} %copy-done.9, f32[1024,256]{1,0:T(8,128)} %copy-done.10, f32[1024,256]{1,0:T(8,128)} %copy-done.2, f32[1024,256]{1,0:T(8,128)} %copy-done.3), custom_call_target="tpu_custom_call" | custom-call | tf_op jit(solution)/shard_map/pallas_call | solution.py:233
  276.6 65.3 %shard_map.48.rest_0_ = f32[3584,512]{1,0:T(8,128)} custom-call(s32[2]{0:T(128)} %copy-done.7, f32[1024,256]{1,0:T(8,128)} %copy-done.11, f32[1024,256]{1,0:T(8,128)} %copy-done.14, f32[1024,256]{1,0:T(8,128)} %copy-done.4, f32[1024,256]{1,0:T(8,128)} %get-tuple-element.21.own_down, f32[3584,512]{1,0:T(8,128)} %shard_map.47.rest_0_), custom_call_target="tpu_custom_call", output_to_operand_aliasing={{}: (5, {})} | custom-call | tf_op jit(solution)/shard_map/pallas_call | solution.py:233
  342.9 65.3 %shard_map.49.rest_0_ = f32[3584,512]{1,0:T(8,128)} custom-call(s32[2]{0:T(128)} %copy-done.7, f32[1024,256]{1,0:T(8,128)} %copy-done.12, f32[1024,256]{1,0:T(8,128)} %collective-permute-done.3.from_right, f32[1024,256]{1,0:T(8,128)} %get-tuple-element.18.own_up, f32[1024,256]{1,0:T(8,128)} %get-tuple-element.19.own_down, ...), custom_call_target="tpu_custom_call", output_to_operand_aliasing={{}: (5, {})} | custom-call | tf_op jit(solution)/shard_map/pallas_call | solution.py:233
  409.2 65.3 %shard_map.50 = f32[3584,512]{1,0:T(8,128)} custom-call(s32[2]{0:T(128)} %copy-done.7, f32[1024,256]{1,0:T(8,128)} %copy-done.13, f32[1024,256]{1,0:T(8,128)} %collective-permute-done.1.from_right, f32[1024,256]{1,0:T(8,128)} %get-tuple-element.16.own_up, f32[1024,256]{1,0:T(8,128)} %get-tuple-element.17.own_down, ...), custom_call_target="tpu_custom_call", output_to_operand_aliasing={{}: (5, {})} | custom-call | tf_op jit(solution)/shard_map/pallas_call | solution.py:233
  (53 shorter events, 12.9 us)
Async XLA Ops:
  9.1 99.4 %slice-start = ((s8[7340032]{0:T(1024)(128)(4,1)}), s8[3145728]{0:T(1024)(128)(4,1)S(1)}, s32[]{:S(2)}) async-start(s8[7340032]{0:T(1024)(128)(4,1)} %bitcast.4), calls=%async_computation.2 | async-start | bytes 6291456
  29.5 15.4 %all-to-all-start.1 = ((f32[8,96,256]{2,1,0:T(8,128)}), f32[8,96,256]{2,1,0:T(8,128)}, u32[]{:S(2)}, u32[]{:S(2)}) async-start(f32[8,96,256]{2,1,0:T(8,128)} %broadcast_in_dim.2), calls=%async_computation.1 | async-start | bytes 1572864 | tf_op jit(solution)/shard_map/all_to_all | solution.py:122
  33.8 70.3 %copy-start.7 = (s32[2]{0:T(128)}, s32[2]{0:T(128)S(1)}, u32[]{:S(2)}) copy-start(s32[2]{0:T(128)S(1)} %add_convert_fusion.swap_ref.ends_ref) | copy-start | bytes 28
  92.1 10.0 %copy-start.8 = (f32[1024,512]{1,0:T(8,128)S(1)}, f32[1024,512]{1,0:T(8,128)}, u32[]{:S(2)}) copy-start(f32[1024,512]{1,0:T(8,128)} %x_ref.11) | copy-start | bytes 6291460
  92.2 16.3 %slice-start.1 = ((s8[7340032]{0:T(1024)(128)(4,1)}), s8[4194304]{0:T(1024)(128)(4,1)S(1)}, s32[]{:S(2)}) async-start(s8[7340032]{0:T(1024)(128)(4,1)} %bitcast.4), calls=%async_computation.3 | async-start | bytes 8388608
  94.9 24.3 %copy-start.4 = (f32[1024,256]{1,0:T(8,128)}, f32[1024,256]{1,0:T(8,128)S(1)}, u32[]{:S(2)}) copy-start(f32[1024,256]{1,0:T(8,128)S(1)} %get-tuple-element.20.own_up) | copy-start | bytes 3145732
  94.9 71.7 %collective-permute-start.4 = (f32[1024,256]{1,0:T(8,128)S(1)}, f32[1024,256]{1,0:T(8,128)S(1)}, u32[]{:S(2)}, u32[]{:S(2)}) collective-permute-start(f32[1024,256]{1,0:T(8,128)S(1)} %get-tuple-element.20.own_up), channel_id=1, source_target_pairs={{0,8},{8,16},{16,24},{24,32},{32,40},{40,48},{48,56},{56,64},{64,7... | collective-permute-start | bytes 3145736 | tf_op jit(solution)/shard_map/ppermute | solution.py:258
  104.1 15.0 %copy-start.2 = (f32[1024,256]{1,0:T(8,128)}, f32[1024,256]{1,0:T(8,128)S(1)}, u32[]{:S(2)}) copy-start(f32[1024,256]{1,0:T(8,128)S(1)} %get-tuple-element.24.own_up) | copy-start | bytes 3145732
  104.1 15.0 %copy-start.3 = (f32[1024,256]{1,0:T(8,128)}, f32[1024,256]{1,0:T(8,128)S(1)}, u32[]{:S(2)}) copy-start(f32[1024,256]{1,0:T(8,128)S(1)} %get-tuple-element.25.own_down) | copy-start | bytes 3145732
  104.1 64.4 %collective-permute-start.8 = (f32[1024,256]{1,0:T(8,128)S(1)}, f32[1024,256]{1,0:T(8,128)S(1)}, u32[]{:S(2)}, u32[]{:S(2)}) collective-permute-start(f32[1024,256]{1,0:T(8,128)S(1)} %get-tuple-element.24.own_up), channel_id=1, source_target_pairs={{0,8},{8,16},{16,24},{24,32},{32,40},{40,48},{48,56},{56,64},{64,7... | collective-permute-start | bytes 3145736 | tf_op jit(solution)/shard_map/ppermute | solution.py:258
  106.1 67.7 %collective-permute-start.9 = (f32[1024,256]{1,0:T(8,128)S(1)}, f32[1024,256]{1,0:T(8,128)S(1)}, u32[]{:S(2)}, u32[]{:S(2)}) collective-permute-start(f32[1024,256]{1,0:T(8,128)S(1)} %get-tuple-element.25.own_down), channel_id=1, source_target_pairs={{8,0},{16,8},{24,16},{32,24},{40,32},{48,40},{56,48},{64,56},{72,6... | collective-permute-start | bytes 3145736 | tf_op jit(solution)/shard_map/ppermute | solution.py:259
  109.5 12.7 %copy-start.5 = (f32[512,256]{1,0:T(8,128)}, f32[512,256]{1,0:T(8,128)S(1)}, u32[]{:S(2)}) copy-start(f32[512,256]{1,0:T(8,128)S(1)} %get-tuple-element.22.own_up) | copy-start | bytes 1572868
  109.5 12.6 %copy-start.6 = (f32[512,256]{1,0:T(8,128)}, f32[512,256]{1,0:T(8,128)S(1)}, u32[]{:S(2)}) copy-start(f32[512,256]{1,0:T(8,128)S(1)} %get-tuple-element.23.own_down) | copy-start | bytes 1572868
  109.5 49.2 %collective-permute-start.6 = (f32[512,256]{1,0:T(8,128)S(1)}, f32[512,256]{1,0:T(8,128)S(1)}, u32[]{:S(2)}, u32[]{:S(2)}) collective-permute-start(f32[512,256]{1,0:T(8,128)S(1)} %get-tuple-element.22.own_up), channel_id=1, source_target_pairs={{0,8},{8,16},{16,24},{24,32},{32,40},{40,48},{48,56},{56,64},{64,7... | collective-permute-start | bytes 1572872 | tf_op jit(solution)/shard_map/ppermute | solution.py:258
  114.2 46.5 %collective-permute-start.7 = (f32[512,256]{1,0:T(8,128)S(1)}, f32[512,256]{1,0:T(8,128)S(1)}, u32[]{:S(2)}, u32[]{:S(2)}) collective-permute-start(f32[512,256]{1,0:T(8,128)S(1)} %get-tuple-element.23.own_down), channel_id=1, source_target_pairs={{8,0},{16,8},{24,16},{32,24},{40,32},{48,40},{56,48},{64,56},{72,6... | collective-permute-start | bytes 1572872 | tf_op jit(solution)/shard_map/ppermute | solution.py:259
  158.8 15.0 %copy-start.15 = (f32[512,256]{1,0:T(8,128)}, f32[512,256]{1,0:T(8,128)S(1)}, u32[]{:S(2)}) copy-start(f32[512,256]{1,0:T(8,128)S(1)} %collective-permute-done.6.from_left) | copy-start | bytes 1572868
  158.8 116.8 %collective-permute-start.5 = (f32[1024,256]{1,0:T(8,128)}, f32[1024,256]{1,0:T(8,128)S(1)}, u32[]{:S(2)}, u32[]{:S(2)}) collective-permute-start(f32[1024,256]{1,0:T(8,128)} %get-tuple-element.21.own_down), channel_id=1, source_target_pairs={{8,0},{16,8},{24,16},{32,24},{40,32},{48,40},{56,48},{64,56},{72,6... | collective-permute-start | bytes 3145736 | tf_op jit(solution)/shard_map/ppermute | solution.py:259
  160.7 13.1 %copy-start.16 = (f32[512,256]{1,0:T(8,128)}, f32[512,256]{1,0:T(8,128)S(1)}, u32[]{:S(2)}) copy-start(f32[512,256]{1,0:T(8,128)S(1)} %collective-permute-done.7.from_right) | copy-start | bytes 1572868
  160.7 181.2 %collective-permute-start.2 = (f32[1024,256]{1,0:T(8,128)}, f32[1024,256]{1,0:T(8,128)S(1)}, u32[]{:S(2)}, u32[]{:S(2)}) collective-permute-start(f32[1024,256]{1,0:T(8,128)} %get-tuple-element.18.own_up), channel_id=1, source_target_pairs={{0,8},{8,16},{16,24},{24,32},{32,40},{40,48},{48,56},{56,64},{64,7... | collective-permute-start | bytes 3145736 | tf_op jit(solution)/shard_map/ppermute | solution.py:258
  166.6 7.2 %copy-start.11 = (f32[1024,256]{1,0:T(8,128)}, f32[1024,256]{1,0:T(8,128)S(1)}, u32[]{:S(2)}) copy-start(f32[1024,256]{1,0:T(8,128)S(1)} %collective-permute-done.4.from_left) | copy-start | bytes 3145732
  166.6 175.3 %collective-permute-start.3 = (f32[1024,256]{1,0:T(8,128)}, f32[1024,256]{1,0:T(8,128)}, u32[]{:S(2)}, u32[]{:S(2)}) collective-permute-start(f32[1024,256]{1,0:T(8,128)} %get-tuple-element.19.own_down), channel_id=1, source_target_pairs={{8,0},{16,8},{24,16},{32,24},{40,32},{48,40},{56,48},{64,56},{72,6... | collective-permute-start | bytes 3145736 | tf_op jit(solution)/shard_map/ppermute | solution.py:259
  168.6 5.2 %copy-start.9 = (f32[1024,256]{1,0:T(8,128)}, f32[1024,256]{1,0:T(8,128)S(1)}, u32[]{:S(2)}) copy-start(f32[1024,256]{1,0:T(8,128)S(1)} %collective-permute-done.8.from_left) | copy-start | bytes 3145732
  168.6 239.7 %collective-permute-start = (f32[1024,256]{1,0:T(8,128)}, f32[1024,256]{1,0:T(8,128)S(1)}, u32[]{:S(2)}, u32[]{:S(2)}) collective-permute-start(f32[1024,256]{1,0:T(8,128)} %get-tuple-element.16.own_up), channel_id=1, source_target_pairs={{0,8},{8,16},{16,24},{24,32},{32,40},{40,48},{48,56},{56,64},{64,7... | collective-permute-start | bytes 3145736 | tf_op jit(solution)/shard_map/ppermute | solution.py:258
  174.8 233.5 %collective-permute-start.1 = (f32[1024,256]{1,0:T(8,128)}, f32[1024,256]{1,0:T(8,128)}, u32[]{:S(2)}, u32[]{:S(2)}) collective-permute-start(f32[1024,256]{1,0:T(8,128)} %get-tuple-element.17.own_down), channel_id=1, source_target_pairs={{8,0},{16,8},{24,16},{32,24},{40,32},{48,40},{56,48},{64,56},{72,6... | collective-permute-start | bytes 3145736 | tf_op jit(solution)/shard_map/ppermute | solution.py:259
  (6 other events, 10.2 us)

commit v2 on v1

--- a/solution.py
+++ b/solution.py
@@ -9,6 +9,7 @@
 
 POLAR_STEPS = 10
 LEAF = 128
+VMEM_ALL = 60 * 2**20
 F32 = jnp.float32
 BF16 = jnp.bfloat16
 NT = (((1,), (1,)), ((), ()))
@@ -109,7 +110,8 @@
         in_specs=[pl.BlockSpec((tile, n), lambda i: (i, 0))],
         out_specs=pl.BlockSpec((3 * half, half), lambda i: (0, 0)),
         scratch_shapes=[pltpu.VMEM((n, n), F32), pltpu.VMEM((n, n), F32)],
-        compiler_params=pltpu.CompilerParams(vmem_limit_bytes=32 * 2**20),
+        compiler_params=pltpu.CompilerParams(vmem_limit_bytes=14 * 2**20),
+        cost_estimate=pl.CostEstimate(flops=1024, bytes_accessed=1024, transcendentals=0),
     )(x)
 
 
@@ -122,7 +124,7 @@
     return lax.all_to_all(spread, "row", 0, 0, tiled=True).reshape(gram.shape)
 
 
-def transform_kernel(swap_ref, gram_ref, hi_ref, lo_ref, work):
+def transform_kernel(swap_ref, gram_ref, inner_ref, outer_ref, work):
     n = work.shape[0]
     half = n // 2
     work[:half, :half] = gram_ref[:half]
@@ -137,13 +139,18 @@
         c = lax.broadcasted_iota(jnp.int32, (LEAF, LEAF), 1)
         lower = jnp.where(c <= r, block, 0.0)
         work[at, at] = (r == c).astype(F32)
-        panel = dot_high(lower, work[at, :])
-        col = lax.broadcasted_iota(jnp.int32, (LEAF, n), 1)
-        scaled = jnp.where(col >= (p + 1) * LEAF, panel * inv[:, :1], 0.0)
-        work[at, :] = panel
-        later = lax.broadcasted_iota(jnp.int32, (n, LEAF), 0) >= (p + 1) * LEAF
-        work[:, at] = jnp.where(later, 0.0, work[:, at])
-        work[...] -= dot_high(scaled, panel, TN)
+        for q in range(n // LEAF):
+
+            @pl.when(p == q)
+            def _():
+                e = (q + 1) * LEAF
+                panel = dot_high(lower, work[q * LEAF : e, :])
+                work[q * LEAF : e, :] = panel
+                if e < n:
+                    scaled = panel[:, e:] * inv[:, :1]
+                    work[e:, q * LEAF : e] = jnp.zeros((n - e, LEAF), F32)
+                    work[e:, :] -= dot_high(scaled, panel, TN)
+
         return carry
 
     lax.fori_loop(0, n // LEAF, block_step, 0)
@@ -162,34 +169,40 @@
         return carry
 
     lax.fori_loop(0, POLAR_STEPS, polar_step, 0)
-    for side in range(2):
+    for side, out in enumerate((inner_ref, outer_ref)):
         begin = pl.multiple_of(jnp.bitwise_xor(swap_ref[0], side) * half, half)
-        hi, lo = split(work[pl.ds(begin, half), :].T)
-        hi_ref[:, side * half : (side + 1) * half] = hi
-        lo_ref[:, side * half : (side + 1) * half] = lo
+        out[...] = work[pl.ds(begin, half), :].T
 
 
 def make_transform(gram, swap):
     n = 2 * gram.shape[1]
     return pl.pallas_call(
         transform_kernel,
-        out_shape=[jax.ShapeDtypeStruct((n, n), BF16)] * 2,
+        out_shape=[jax.ShapeDtypeStruct((n, n // 2), F32)] * 2,
         in_specs=[pl.BlockSpec(memory_space=pltpu.SMEM), pl.BlockSpec(memory_space=pltpu.VMEM)],
         out_specs=[pl.BlockSpec(memory_space=pltpu.VMEM)] * 2,
         scratch_shapes=[pltpu.VMEM((n, n), F32)],
-        compiler_params=pltpu.CompilerParams(vmem_limit_bytes=48 * 2**20),
+        compiler_params=pltpu.CompilerParams(vmem_limit_bytes=16 * 2**20),
+        cost_estimate=pl.CostEstimate(flops=1024, bytes_accessed=1024, transcendentals=0),
     )(swap, gram)
 
 
-def apply_kernel(x_ref, hi_ref, lo_ref, up_ref, down_ref):
-    half = up_ref.shape[1]
-    xs = split(x_ref[...])
-    both = dot3(xs, (hi_ref[...], lo_ref[...]))
-    up_ref[...] = both[:, :half]
-    down_ref[...] = both[:, half:]
-
-
-def apply_rows(x, begin, rows, parts, tile=512):
+def apply_kernel(x_ref, t_inner, t_outer, inner_ref, outer_ref, parts):
+    half = inner_ref.shape[1]
+
+    @pl.when(pl.program_id(0) == 0)
+    def _():
+        for side, t in enumerate((t_inner, t_outer)):
+            hi, lo = split(t[...])
+            parts[0, :, side * half : (side + 1) * half] = hi
+            parts[1, :, side * half : (side + 1) * half] = lo
+
+    both = dot3(split(x_ref[...]), (parts[0], parts[1]))
+    inner_ref[...] = both[:, :half]
+    outer_ref[...] = both[:, half:]
+
+
+def apply_rows(x, begin, rows, turns, tile=512):
     n = x.shape[1]
     half = n // 2
     first = begin // tile
@@ -199,67 +212,123 @@
         out_shape=[jax.ShapeDtypeStruct((rows, half), F32)] * 2,
         in_specs=[
             pl.BlockSpec((tile, n), lambda i: (first + i, 0)),
-            pl.BlockSpec((n, n), lambda i: (0, 0)),
-            pl.BlockSpec((n, n), lambda i: (0, 0)),
+            pl.BlockSpec((n, half), lambda i: (0, 0)),
+            pl.BlockSpec((n, half), lambda i: (0, 0)),
         ],
         out_specs=[pl.BlockSpec((tile, half), lambda i: (i, 0))] * 2,
-        compiler_params=pltpu.CompilerParams(vmem_limit_bytes=32 * 2**20),
+        scratch_shapes=[pltpu.VMEM((2, n, n), BF16)],
+        compiler_params=pltpu.CompilerParams(vmem_limit_bytes=14 * 2**20),
         cost_estimate=pl.CostEstimate(flops=6 * rows * n * n, bytes_accessed=8 * rows * n, transcendentals=0),
-    )(x, *parts)
-
-
-def place_kernel(begin, ends_ref, from_left, from_right, own_up, own_down, *rest):
-    out, sems = rest[-2], rest[-1]
-    rows, half = from_left.shape
-    at = pl.ds(begin, rows)
-    for side, (own, other) in enumerate(((own_down, from_left), (own_up, from_right))):
-        target = out.at[at, pl.ds(side * half, half)]
-
-        @pl.when(ends_ref[side] == 1)
-        def _():
-            pltpu.make_async_copy(own, target, sems.at[side]).start()
-
-        @pl.when(ends_ref[side] == 0)
-        def _():
-            pltpu.make_async_copy(other, target, sems.at[side]).start()
-
-    for side in range(2):
-        target = out.at[at, pl.ds(side * half, half)]
-        pltpu.make_async_copy(from_left, target, sems.at[side]).wait()
-
-
-def place_rows(out, shape, begin, ends, blocks):
-    args = [ends, *blocks] + ([] if out is None else [out])
-    return pl.pallas_call(
-        functools.partial(place_kernel, begin),
+    )(x, *turns)
+
+
+def arrived_kernel(core_ref, inner, outer, t_inner, t_outer, *rest):
+    out, parts = rest[-2], rest[-1]
+    half = t_inner.shape[1]
+
+    @pl.when(pl.program_id(0) == 0)
+    def _():
+        for side, t in enumerate((t_inner, t_outer)):
+            hi, lo = split(t[...])
+            parts[side, 0] = hi
+            parts[side, 1] = lo
+
+    for side, block in enumerate((inner, outer)):
+        at = pl.ds(pl.multiple_of(jnp.bitwise_xor(core_ref[0], 1 - side) * half, half), half)
+        out[:, at] = dot3(split(block[...]), (parts[side, 0], parts[side, 1]))
+
+
+def arrived_rows(out, shape, begin, rows, core, blocks, skip, turns, tile=512):
+    n = shape[1]
+    first, here = begin // tile, skip // tile
+    args = [core, *blocks, *turns] + ([] if out is None else [out])
+    return pl.pallas_call(
+        arrived_kernel,
+        grid=(rows // tile,),
+        in_specs=[
+            pl.BlockSpec(memory_space=pltpu.SMEM),
+            pl.BlockSpec((tile, n), lambda i: (here + i, 0)),
+            pl.BlockSpec((tile, n), lambda i: (here + i, 0)),
+            pl.BlockSpec((n, n // 2), lambda i: (0, 0)),
+            pl.BlockSpec((n, n // 2), lambda i: (0, 0)),
+        ]
+        + [pl.BlockSpec(memory_space=pl.ANY)] * (len(args) - 5),
+        out_specs=pl.BlockSpec((tile, n), lambda i: (first + i, 0)),
+        scratch_shapes=[pltpu.VMEM((2, 2, n, n // 2), BF16)],
         out_shape=jax.ShapeDtypeStruct(shape, F32),
-        in_specs=[pl.BlockSpec(memory_space=pltpu.SMEM)] + [pl.BlockSpec(memory_space=pl.ANY)] * (len(args) - 1),
-        out_specs=pl.BlockSpec(memory_space=pl.ANY),
-        scratch_shapes=[pltpu.SemaphoreType.DMA((2,))],
         input_output_aliases={} if out is None else {len(args) - 1: 0},
+        compiler_params=pltpu.CompilerParams(vmem_limit_bytes=24 * 2**20),
+        cost_estimate=pl.CostEstimate(flops=6 * rows * n * n, bytes_accessed=8 * rows * n, transcendentals=0),
     )(*args)
 
 
-CHUNKS = ((0, 0, 512), (0, 512, 1024), (0, 1536, 1024), (1, 0, 1024), (0, 2560, 1024))
+def place_kernel(core_ref, inner, outer, *rest):
+    out = rest[-1]
+    half = inner.shape[1]
+    for side, block in enumerate((inner, outer)):
+        at = pl.ds(pl.multiple_of(jnp.bitwise_xor(core_ref[0], 1 - side) * half, half), half)
+        out[:, at] = block[...]
+
+
+def place_rows(out, shape, begin, core, blocks, tile=512):
+    rows, half = blocks[0].shape
+    first = begin // tile
+    args = [core, *blocks] + ([] if out is None else [out])
+    return pl.pallas_call(
+        place_kernel,
+        grid=(rows // tile,),
+        in_specs=[pl.BlockSpec(memory_space=pltpu.SMEM)]
+        + [pl.BlockSpec((tile, half), lambda i: (i, 0))] * 2
+        + [pl.BlockSpec(memory_space=pl.ANY)] * (len(args) - 3),
+        out_specs=pl.BlockSpec((tile, 2 * half), lambda i: (first + i, 0)),
+        out_shape=jax.ShapeDtypeStruct(shape, F32),
+        input_output_aliases={} if out is None else {len(args) - 1: 0},
+        compiler_params=pltpu.CompilerParams(vmem_limit_bytes=8 * 2**20),
+        cost_estimate=pl.CostEstimate(flops=1024, bytes_accessed=16 * rows * half, transcendentals=0),
+    )(*args)
+
+
+EARLY = ((1, 0, 1024),)
+LATE = ((0, 0, 1024), (0, 1024, 1024), (0, 2048, 1024), (0, 3072, 512))
+
+
+def raw_rows(sources):
+    blocks = [lax.slice_in_dim(sources[w], begin, begin + rows) for w, begin, rows in EARLY]
+    return blocks[0] if len(blocks) == 1 else jnp.concatenate(blocks)
 
 
 def on_device(matrix, vectors):
-    count_col = lax.axis_size("col")
+    count = lax.axis_size("col")
     own_index = lax.axis_index("col")
-    ends = jnp.stack([own_index == 0, own_index == count_col - 1]).astype(jnp.int32)
-    upward = [(i, i + 1) for i in range(count_col - 1)]
-    downward = [(i + 1, i) for i in range(count_col - 1)]
+    core = jnp.reshape(own_index % 2, (1,)).astype(jnp.int32)
+    within = [(i, i ^ 1) for i in range(count)]
+    across = [(0, 0), (count - 1, count - 1)]
+    across += [(i, i + 1) for i in range(1, count - 1, 2)] + [(i + 1, i) for i in range(1, count - 1, 2)]
+    swap = jnp.where(own_index == 0, 1, core).astype(jnp.int32)
     sources = (matrix, vectors)
     results = [None, None]
+
+    def pass_on(inner, outer):
+        return lax.ppermute(inner, "col", within), lax.ppermute(outer, "col", across)
+
     gram = sum_over_rows(make_gram(matrix))
-    parts = make_transform(gram, ends)
-    for which, begin, rows in CHUNKS:
-        up, down = apply_rows(sources[which], begin, rows, parts)
-        from_left = lax.ppermute(up, "col", upward)
-        from_right = lax.ppermute(down, "col", downward)
-        results[which] = place_rows(
-            results[which], sources[which].shape, begin, ends, (from_left, from_right, up, down)
+    raw, gram = lax.optimization_barrier((raw_rows(sources), gram))
+    early = pass_on(raw, raw)
+    own_turns = make_transform(gram, swap)
+    waits = [early, pass_on(*own_turns)]
+    for which, begin, rows in LATE:
+        blocks = apply_rows(sources[which], begin, rows, own_turns)
+        blocks, waits[-2] = lax.optimization_barrier((blocks, waits[-2]))
+        waits.append(pass_on(*blocks))
+    early, turns = waits[:2]
+    skip = 0
+    for which, begin, rows in EARLY:
+        results[which] = arrived_rows(
+            results[which], sources[which].shape, begin, rows, core, early, skip, turns
         )
+        skip += rows
+    for (which, begin, rows), blocks in zip(LATE, waits[2:]):
+        results[which] = place_rows(results[which], sources[which].shape, begin, core, blocks)
     return tuple(results)
 
 

time: 476 us -> 186 us (0.39)
  Pallas kernels: 356 us -> 60.4 us
  blocking collectives: 18.3 us -> 31 us
  waiting for transfers between devices: 47.7 us -> 59.8 us
  starting transfers between devices: 39.1 us -> 27.6 us
  local copies, waits for them, and re-layouts: 11.1 us -> 6.22 us
    pallas_call x6, Pallas kernels: 339 us -> 47.6 us  [the longest x1 37.9 us: make_transform(): pl.pallas_call(transform_kernel, out_shape=[jax.ShapeDtypeStruct((n, n //...]
    ppermute x10 -> x12, waiting for transfers between devices: 36.6 us -> 59.8 us  [the longest x6 59.8 us: pass_on(): lax.ppermute(outer, 'col', across)]
    all_to_all x0 -> x1, blocking collectives: none -> 13.1 us  [sum_over_rows(): return lax.all_to_all(spread, 'row', 0, 0, tiled=True).reshape(gram.shape)]
    all_to_all x1 -> x0, waiting for transfers between devices: 11.1 us -> none  [sum_over_rows(): return lax.all_to_all(spread, 'row', 0, 0, tiled=True).reshape(gram.shape)]
    ppermute x10 -> x12, starting transfers between devices: 34.9 us -> 27.6 us  [the longest x6 26.2 us: pass_on(): lax.ppermute(outer, 'col', across)]
    pallas_call x5 -> x4, Pallas kernels: 11.8 us -> 7.49 us  [apply_rows(): pl.pallas_call(apply_kernel, grid=(rows // tile,), out_shape=[jax.ShapeDt...]
    unnamed x38 -> x4, local copies, waits for them, and re-layouts: 10.2 us -> 6.16 us
  transfers between devices with their start and end apart: 11 -> 12, of which waited for: 2 -> 5; matrix products, arithmetic and copies ran while one was open for 0% -> 0% of each run, Pallas kernels for 50% -> 29%
where the time goes in v2:
time: 186 us
  Pallas kernels  60.4 us (32%)
  waiting for transfers between devices  59.8 us (32%)
  blocking collectives  31 us (17%)
  starting transfers between devices  27.6 us (15%)
  local copies, waits for them, and re-layouts  6.22 us (3%)
    ppermute x6, waiting for transfers between devices, pass_on(): lax.ppermute(outer, 'col', across)  59.8 us
    pallas_call x1, Pallas kernels, make_transform(): pl.pallas_call(transform_kernel, out_shape=[jax.ShapeDtypeStruct((n, n //...  37.9 us
    ppermute x6, starting transfers between devices, pass_on(): lax.ppermute(outer, 'col', across)  26.2 us
    all_to_all x1, blocking collectives, sum_over_rows(): theirs = lax.all_to_all(pieces, 'row', 0, 0, tiled=True)  17.9 us
    all_to_all x1, blocking collectives, sum_over_rows(): return lax.all_to_all(spread, 'row', 0, 0, tiled=True).reshape(gram.shape)  13.1 us
    pallas_call x4, Pallas kernels, apply_rows(): pl.pallas_call(apply_kernel, grid=(rows // tile,), out_shape=[jax.ShapeDt...  7.49 us
    unnamed x4, local copies, waits for them, and re-layouts  6.16 us
    pallas_call x1, Pallas kernels, make_gram(): pl.pallas_call(gram_kernel, grid=(rows // tile,), out_shape=jax.ShapeDtyp...  5.31 us
  transfers between devices with their start and end apart: 12, of which 5 were waited for; matrix products, arithmetic and copies ran while one was open for 0% of the time, Pallas kernels for 29%

profile of v2, /device:TPU:3, one launch (start us, length us, event | category | flops | bytes accessed | tf_op | source)
XLA Modules:
  0.0 185.8 jit_solution(946925720602596508)
XLA Ops:
  0.6 3.1 %copy-done = f32[3584,512]{1,0:T(8,128)S(1)} copy-done((f32[3584,512]{1,0:T(8,128)S(1)}, f32[3584,512]{1,0:T(8,128)}, u32[]{:S(2)}) %copy-start) | copy-done | bytes 7340056
  3.7 5.3 %shard_map.41 = f32[768,256]{1,0:T(8,128)S(1)} custom-call(f32[3584,512]{1,0:T(8,128)S(1)} %copy-done), custom_call_target="tpu_custom_call" | custom-call | flops 1024 | bytes 1024 | tf_op jit(solution)/shard_map/pallas_call | solution.py:106
  9.0 17.9 %all_to_all.10 = f32[8,96,256]{2,1,0:T(8,128)S(1)} all-to-all(f32[8,96,256]{2,1,0:T(8,128)S(1)} %bitcast.5), channel_id=1, replica_groups=mesh['col'=16,'row'=8] {'row'}, dimensions={0} | all-to-all | bytes 1572864 | tf_op jit(solution)/shard_map/all_to_all | solution.py:121
  27.1 13.1 %all_to_all.11 = f32[8,96,256]{2,1,0:T(8,128)S(1)} all-to-all(f32[8,96,256]{2,1,0:T(8,128)S(1)} %broadcast_in_dim.4), channel_id=1, replica_groups=mesh['col'=16,'row'=8] {'row'}, dimensions={0} | all-to-all | bytes 1572864 | tf_op jit(solution)/shard_map/all_to_all | solution.py:124
  40.1 7.6 %collective-permute-start.7 = (f32[1024,512]{1,0:T(8,128)}, f32[1024,512]{1,0:T(8,128)S(1)}, u32[]{:S(2)}, u32[]{:S(2)}) collective-permute-start(f32[1024,512]{1,0:T(8,128)} %param.3), channel_id=1, source_target_pairs={{0,0},{120,120},{8,16},{24,32},{40,48},{56,64},{72,80},{88,96},{10... | collective-permute-start | bytes 6291464 | tf_op jit(solution)/shard_map/ppermute | solution.py:312
  47.9 37.9 %shard_map.42 = (f32[512,256]{1,0:T(8,128)S(1)}, f32[512,256]{1,0:T(8,128)S(1)}) custom-call(s32[1]{0:T(128)S(6)} %select_n.17.swap_ref, f32[768,256]{1,0:T(8,128)S(1)} %bitcast.4), custom_call_target="tpu_custom_call" | custom-call | flops 1024 | bytes 1024 | tf_op jit(solution)/shard_map/pallas_call | solution.py:179
  86.3 3.1 %collective-permute-start.1 = (f32[512,256]{1,0:T(8,128)S(1)}, f32[512,256]{1,0:T(8,128)S(1)}, u32[]{:S(2)}, u32[]{:S(2)}) collective-permute-start(f32[512,256]{1,0:T(8,128)S(1)} %get-tuple-element.32.t_outer), channel_id=1, source_target_pairs={{0,0},{120,120},{8,16},{24,32},{40,48},{56,64},{72,80},{88,96},{10... | collective-permute-start | bytes 1572872 | tf_op jit(solution)/shard_map/ppermute | solution.py:312
  89.4 3.1 %copy-done.1 = f32[3584,512]{1,0:T(8,128)S(1)} copy-done((f32[3584,512]{1,0:T(8,128)S(1)}, f32[3584,512]{1,0:T(8,128)}, u32[]{:S(2)}) %copy-start.1) | copy-done | bytes 7340056
  92.5 2.2 %shard_map.46 = (f32[1024,256]{1,0:T(8,128)S(1)}, f32[1024,256]{1,0:T(8,128)S(1)}) custom-call(f32[3584,512]{1,0:T(8,128)S(1)} %copy-done.1, f32[512,256]{1,0:T(8,128)S(1)} %get-tuple-element.31.t_inner, f32[512,256]{1,0:T(8,128)S(1)} %get-tuple-element.32.t_outer), custom_call_target="tpu_custom_call" | custom-call | flops 1610612736 | bytes 4194304 | tf_op jit(solution)/shard_map/pallas_call | solution.py:209
  94.7 5.1 %collective-permute-done.7.outer = f32[1024,512]{1,0:T(8,128)S(1)} collective-permute-done((f32[1024,512]{1,0:T(8,128)}, f32[1024,512]{1,0:T(8,128)S(1)}, u32[]{:S(2)}, u32[]{:S(2)}) %collective-permute-start.7) | collective-permute-done | bytes 2097184 | tf_op jit(solution)/shard_map/ppermute | solution.py:312
  99.8 3.8 %collective-permute-start.9 = (f32[1024,256]{1,0:T(8,128)S(1)}, f32[1024,256]{1,0:T(8,128)S(1)}, u32[]{:S(2)}, u32[]{:S(2)}) collective-permute-start(f32[1024,256]{1,0:T(8,128)S(1)} %get-tuple-element.47), channel_id=1, source_target_pairs={{0,0},{120,120},{8,16},{24,32},{40,48},{56,64},{72,80},{88,96},{10... | collective-permute-start | bytes 3145736 | tf_op jit(solution)/shard_map/ppermute | solution.py:312
  103.5 2.2 %shard_map.44 = (f32[1024,256]{1,0:T(8,128)S(1)}, f32[1024,256]{1,0:T(8,128)S(1)}) custom-call(f32[3584,512]{1,0:T(8,128)S(1)} %copy-done.1, f32[512,256]{1,0:T(8,128)S(1)} %get-tuple-element.31.t_inner, f32[512,256]{1,0:T(8,128)S(1)} %get-tuple-element.32.t_outer), custom_call_target="tpu_custom_call" | custom-call | flops 1610612736 | bytes 4194304 | tf_op jit(solution)/shard_map/pallas_call | solution.py:209
  106.5 4.2 %collective-permute-start.3 = (f32[1024,256]{1,0:T(8,128)S(1)}, f32[1024,256]{1,0:T(8,128)S(1)}, u32[]{:S(2)}, u32[]{:S(2)}) collective-permute-start(f32[1024,256]{1,0:T(8,128)S(1)} %get-tuple-element.38), channel_id=1, source_target_pairs={{0,0},{120,120},{8,16},{24,32},{40,48},{56,64},{72,80},{88,96},{10... | collective-permute-start | bytes 3145736 | tf_op jit(solution)/shard_map/ppermute | solution.py:312
  110.7 2.2 %shard_map.45 = (f32[1024,256]{1,0:T(8,128)S(1)}, f32[1024,256]{1,0:T(8,128)S(1)}) custom-call(f32[3584,512]{1,0:T(8,128)S(1)} %copy-done.1, f32[512,256]{1,0:T(8,128)S(1)} %get-tuple-element.31.t_inner, f32[512,256]{1,0:T(8,128)S(1)} %get-tuple-element.32.t_outer), custom_call_target="tpu_custom_call" | custom-call | flops 1610612736 | bytes 4194304 | tf_op jit(solution)/shard_map/pallas_call | solution.py:209
  112.9 26.9 %collective-permute-done.9.outer = f32[1024,256]{1,0:T(8,128)S(1)} collective-permute-done((f32[1024,256]{1,0:T(8,128)S(1)}, f32[1024,256]{1,0:T(8,128)S(1)}, u32[]{:S(2)}, u32[]{:S(2)}) %collective-permute-start.9) | collective-permute-done | bytes 1048608 | tf_op jit(solution)/shard_map/ppermute | solution.py:312
  139.8 3.7 %collective-permute-start.11 = (f32[1024,256]{1,0:T(8,128)S(1)}, f32[1024,256]{1,0:T(8,128)S(1)}, u32[]{:S(2)}, u32[]{:S(2)}) collective-permute-start(f32[1024,256]{1,0:T(8,128)S(1)} %get-tuple-element.49), channel_id=1, source_target_pairs={{0,0},{120,120},{8,16},{24,32},{40,48},{56,64},{72,80},{88,96},{10... | collective-permute-start | bytes 3145736 | tf_op jit(solution)/shard_map/ppermute | solution.py:312
  144.6 17.7 %collective-permute-done.3.outer = f32[1024,256]{1,0:T(8,128)S(1)} collective-permute-done((f32[1024,256]{1,0:T(8,128)S(1)}, f32[1024,256]{1,0:T(8,128)S(1)}, u32[]{:S(2)}, u32[]{:S(2)}) %collective-permute-start.3) | collective-permute-done | bytes 1048608 | tf_op jit(solution)/shard_map/ppermute | solution.py:312
  162.3 3.7 %collective-permute-start.5 = (f32[512,256]{1,0:T(8,128)S(1)}, f32[512,256]{1,0:T(8,128)S(1)}, u32[]{:S(2)}, u32[]{:S(2)}) collective-permute-start(f32[512,256]{1,0:T(8,128)S(1)} %get-tuple-element.40), channel_id=1, source_target_pairs={{0,0},{120,120},{8,16},{24,32},{40,48},{56,64},{72,80},{88,96},{10... | collective-permute-start | bytes 1572872 | tf_op jit(solution)/shard_map/ppermute | solution.py:312
  166.1 4.5 %shard_map.51 = f32[1024,512]{1,0:T(8,128)} custom-call(s32[1]{0:T(128)} %bitcast.core_ref, f32[1024,512]{1,0:T(8,128)} %collective-permute-done.6.inner, f32[1024,512]{1,0:T(8,128)S(1)} %collective-permute-done.7.outer, f32[512,256]{1,0:T(8,128)S(1)} %collective-permute-done.t_inner, f32[512,256]{1,0:T(8,128)S(1)} %collective-permute-done.1.t_outer), custom_call_target="tpu_custom_call" | custom-call | flops 1610612736 | bytes 4194304 | tf_op jit(solution)/shard_map/pallas_call | solution.py:245
  170.5 1.4 shard_map.47.rest_0_
  171.9 1.4 shard_map.48.rest_0_
  173.3 5.8 %collective-permute-done.11.outer = f32[1024,256]{1,0:T(8,128)S(1)} collective-permute-done((f32[1024,256]{1,0:T(8,128)S(1)}, f32[1024,256]{1,0:T(8,128)S(1)}, u32[]{:S(2)}, u32[]{:S(2)}) %collective-permute-start.11) | collective-permute-done | bytes 1048608 | tf_op jit(solution)/shard_map/ppermute | solution.py:312
  179.2 1.4 shard_map.49.rest_0_
  180.6 4.2 %collective-permute-done.5.outer = f32[512,256]{1,0:T(8,128)S(1)} collective-permute-done((f32[512,256]{1,0:T(8,128)S(1)}, f32[512,256]{1,0:T(8,128)S(1)}, u32[]{:S(2)}, u32[]{:S(2)}) %collective-permute-start.5) | collective-permute-done | bytes 524320 | tf_op jit(solution)/shard_map/ppermute | solution.py:312
  (19 shorter events, 3.6 us)
Async XLA Ops:
  0.6 3.1 %copy-start = (f32[3584,512]{1,0:T(8,128)S(1)}, f32[3584,512]{1,0:T(8,128)}, u32[]{:S(2)}) copy-start(f32[3584,512]{1,0:T(8,128)} %x_ref.9) | copy-start | bytes 22020100
  40.1 59.6 %collective-permute-start.7 = (f32[1024,512]{1,0:T(8,128)}, f32[1024,512]{1,0:T(8,128)S(1)}, u32[]{:S(2)}, u32[]{:S(2)}) collective-permute-start(f32[1024,512]{1,0:T(8,128)} %param.3), channel_id=1, source_target_pairs={{0,0},{120,120},{8,16},{24,32},{40,48},{56,64},{72,80},{88,96},{10... | collective-permute-start | bytes 6291464 | tf_op jit(solution)/shard_map/ppermute | solution.py:312
  47.7 52.0 %collective-permute-start.6 = (f32[1024,512]{1,0:T(8,128)}, f32[1024,512]{1,0:T(8,128)}, u32[]{:S(2)}, u32[]{:S(2)}) collective-permute-start(f32[1024,512]{1,0:T(8,128)} %param.3), channel_id=1, source_target_pairs={{0,8},{8,0},{16,24},{24,16},{32,40},{40,32},{48,56},{56,48},{64,72... | collective-permute-start | bytes 6291464 | tf_op jit(solution)/shard_map/ppermute | solution.py:312
  85.8 19.9 %collective-permute-start = (f32[512,256]{1,0:T(8,128)S(1)}, f32[512,256]{1,0:T(8,128)S(1)}, u32[]{:S(2)}, u32[]{:S(2)}) collective-permute-start(f32[512,256]{1,0:T(8,128)S(1)} %get-tuple-element.31.t_inner), channel_id=1, source_target_pairs={{0,8},{8,0},{16,24},{24,16},{32,40},{40,32},{48,56},{56,48},{64,72... | collective-permute-start | bytes 1572872 | tf_op jit(solution)/shard_map/ppermute | solution.py:312
  86.3 19.4 %collective-permute-start.1 = (f32[512,256]{1,0:T(8,128)S(1)}, f32[512,256]{1,0:T(8,128)S(1)}, u32[]{:S(2)}, u32[]{:S(2)}) collective-permute-start(f32[512,256]{1,0:T(8,128)S(1)} %get-tuple-element.32.t_outer), channel_id=1, source_target_pairs={{0,0},{120,120},{8,16},{24,32},{40,48},{56,64},{72,80},{88,96},{10... | collective-permute-start | bytes 1572872 | tf_op jit(solution)/shard_map/ppermute | solution.py:312
  89.4 3.1 %copy-start.1 = (f32[3584,512]{1,0:T(8,128)S(1)}, f32[3584,512]{1,0:T(8,128)}, u32[]{:S(2)}) copy-start(f32[3584,512]{1,0:T(8,128)} %x_ref.9) | copy-start | bytes 22020100
  99.7 13.2 %collective-permute-start.8 = (f32[1024,256]{1,0:T(8,128)S(1)}, f32[1024,256]{1,0:T(8,128)S(1)}, u32[]{:S(2)}, u32[]{:S(2)}) collective-permute-start(f32[1024,256]{1,0:T(8,128)S(1)} %get-tuple-element.46), channel_id=1, source_target_pairs={{0,8},{8,0},{16,24},{24,16},{32,40},{40,32},{48,56},{56,48},{64,72... | collective-permute-start | bytes 3145736 | tf_op jit(solution)/shard_map/ppermute | solution.py:312
  99.8 40.1 %collective-permute-start.9 = (f32[1024,256]{1,0:T(8,128)S(1)}, f32[1024,256]{1,0:T(8,128)S(1)}, u32[]{:S(2)}, u32[]{:S(2)}) collective-permute-start(f32[1024,256]{1,0:T(8,128)S(1)} %get-tuple-element.47), channel_id=1, source_target_pairs={{0,0},{120,120},{8,16},{24,32},{40,48},{56,64},{72,80},{88,96},{10... | collective-permute-start | bytes 3145736 | tf_op jit(solution)/shard_map/ppermute | solution.py:312
  105.7 38.9 %collective-permute-start.2 = (f32[1024,256]{1,0:T(8,128)S(1)}, f32[1024,256]{1,0:T(8,128)S(1)}, u32[]{:S(2)}, u32[]{:S(2)}) collective-permute-start(f32[1024,256]{1,0:T(8,128)S(1)} %get-tuple-element.37), channel_id=1, source_target_pairs={{0,8},{8,0},{16,24},{24,16},{32,40},{40,32},{48,56},{56,48},{64,72... | collective-permute-start | bytes 3145736 | tf_op jit(solution)/shard_map/ppermute | solution.py:312
  106.5 55.8 %collective-permute-start.3 = (f32[1024,256]{1,0:T(8,128)S(1)}, f32[1024,256]{1,0:T(8,128)S(1)}, u32[]{:S(2)}, u32[]{:S(2)}) collective-permute-start(f32[1024,256]{1,0:T(8,128)S(1)} %get-tuple-element.38), channel_id=1, source_target_pairs={{0,0},{120,120},{8,16},{24,32},{40,48},{56,64},{72,80},{88,96},{10... | collective-permute-start | bytes 3145736 | tf_op jit(solution)/shard_map/ppermute | solution.py:312
  139.8 33.5 %collective-permute-start.10 = (f32[1024,256]{1,0:T(8,128)S(1)}, f32[1024,256]{1,0:T(8,128)S(1)}, u32[]{:S(2)}, u32[]{:S(2)}) collective-permute-start(f32[1024,256]{1,0:T(8,128)S(1)} %get-tuple-element.48), channel_id=1, source_target_pairs={{0,8},{8,0},{16,24},{24,16},{32,40},{40,32},{48,56},{56,48},{64,72... | collective-permute-start | bytes 3145736 | tf_op jit(solution)/shard_map/ppermute | solution.py:312
  139.8 39.3 %collective-permute-start.11 = (f32[1024,256]{1,0:T(8,128)S(1)}, f32[1024,256]{1,0:T(8,128)S(1)}, u32[]{:S(2)}, u32[]{:S(2)}) collective-permute-start(f32[1024,256]{1,0:T(8,128)S(1)} %get-tuple-element.49), channel_id=1, source_target_pairs={{0,0},{120,120},{8,16},{24,32},{40,48},{56,64},{72,80},{88,96},{10... | collective-permute-start | bytes 3145736 | tf_op jit(solution)/shard_map/ppermute | solution.py:312
  162.3 18.3 %collective-permute-start.4 = (f32[512,256]{1,0:T(8,128)S(1)}, f32[512,256]{1,0:T(8,128)S(1)}, u32[]{:S(2)}, u32[]{:S(2)}) collective-permute-start(f32[512,256]{1,0:T(8,128)S(1)} %get-tuple-element.39), channel_id=1, source_target_pairs={{0,8},{8,0},{16,24},{24,16},{32,40},{40,32},{48,56},{56,48},{64,72... | collective-permute-start | bytes 1572872 | tf_op jit(solution)/shard_map/ppermute | solution.py:312
  162.3 22.5 %collective-permute-start.5 = (f32[512,256]{1,0:T(8,128)S(1)}, f32[512,256]{1,0:T(8,128)S(1)}, u32[]{:S(2)}, u32[]{:S(2)}) collective-permute-start(f32[512,256]{1,0:T(8,128)S(1)} %get-tuple-element.40), channel_id=1, source_target_pairs={{0,0},{120,120},{8,16},{24,32},{40,48},{56,64},{72,80},{88,96},{10... | collective-permute-start | bytes 1572872 | tf_op jit(solution)/shard_map/ppermute | solution.py:312

commit v3 on v2

--- a/solution.py
+++ b/solution.py
@@ -10,6 +10,10 @@
 POLAR_STEPS = 10
 LEAF = 128
 VMEM_ALL = 60 * 2**20
+BLOCKS = 4
+UPPER = tuple((i, j) for i in range(BLOCKS) for j in range(i, BLOCKS))
+PIECES = 4
+DEPTH = 2
 F32 = jnp.float32
 BF16 = jnp.bfloat16
 NT = (((1,), (1,)), ((), ()))
@@ -78,59 +82,82 @@
     return jnp.concatenate(rows, axis=0), jnp.concatenate(inv_pivot, axis=0)
 
 
-def gram_kernel(x_ref, out_ref, same, cross):
-    step = pl.program_id(0)
-    half = x_ref.shape[1] // 2
-
-    @pl.when(step == 0)
-    def _():
-        same[...] = jnp.zeros_like(same)
-        cross[...] = jnp.zeros_like(cross)
-
-    hi, lo = split(x_ref[...])
+def gram_kernel(cuts, x_hbm, out_ref, x, same, cross, sems):
+    half = x.shape[1] // 2
+    copies = []
+    for k, (begin, end) in enumerate(zip(cuts[:-1], cuts[1:])):
+        at = pl.ds(begin, end - begin)
+        copies.append(pltpu.make_async_copy(x_hbm.at[at], x.at[at], sems.at[k]))
+        copies[-1].start()
     dot = functools.partial(lax.dot_general, dimension_numbers=TN, preferred_element_type=F32)
-    same[:half, :] += dot(hi[:, :half], hi)
-    same[half:, half:] += dot(hi[:, half:], hi[:, half:])
-    cross[...] += dot(hi, lo)
-
-    @pl.when(step == pl.num_programs(0) - 1)
-    def _():
-        out_ref[:half] = same[:half, :half] + (cross[:half, :half] + cross[:half, :half].T)
-        out_ref[half : 2 * half] = same[:half, half:] + (cross[:half, half:] + cross[half:, :half].T)
-        out_ref[2 * half :] = same[half:, half:] + (cross[half:, half:] + cross[half:, half:].T)
-
-
-def make_gram(x, tile=512):
+    for k, (begin, end) in enumerate(zip(cuts[:-1], cuts[1:])):
+        copies[k].wait()
+        hi, lo = split(x[begin:end])
+        first, last, mixed = dot(hi[:, :half], hi), dot(hi[:, half:], hi[:, half:]), dot(hi, lo)
+        if k == 0:
+            same[:half, :] = first
+            same[half:, half:] = last
+            cross[...] = mixed
+        else:
+            same[:half, :] += first
+            same[half:, half:] += last
+            cross[...] += mixed
+    for k, (i, j) in enumerate(UPPER):
+        rows, cols = slice(i * LEAF, (i + 1) * LEAF), slice(j * LEAF, (j + 1) * LEAF)
+        out_ref[k * LEAF : (k + 1) * LEAF] = same[rows, cols] + (cross[rows, cols] + cross[cols, rows].T)
+
+
+def make_gram(x):
     rows, n = x.shape
-    half = n // 2
-    return pl.pallas_call(
-        gram_kernel,
-        grid=(rows // tile,),
-        out_shape=jax.ShapeDtypeStruct((3 * half, half), F32),
-        in_specs=[pl.BlockSpec((tile, n), lambda i: (i, 0))],
-        out_specs=pl.BlockSpec((3 * half, half), lambda i: (0, 0)),
-        scratch_shapes=[pltpu.VMEM((n, n), F32), pltpu.VMEM((n, n), F32)],
-        compiler_params=pltpu.CompilerParams(vmem_limit_bytes=14 * 2**20),
+    size = (len(UPPER) * LEAF, LEAF)
+    cuts = (0, rows // 7, 3 * rows // 7, rows)
+    return pl.pallas_call(
+        functools.partial(gram_kernel, cuts),
+        out_shape=jax.ShapeDtypeStruct(size, F32),
+        in_specs=[pl.BlockSpec(memory_space=pl.ANY)],
+        out_specs=pl.BlockSpec(memory_space=pltpu.VMEM),
+        scratch_shapes=[
+            pltpu.VMEM((rows, n), F32),
+            pltpu.VMEM((n, n), F32),
+            pltpu.VMEM((n, n), F32),
+            pltpu.SemaphoreType.DMA((len(cuts) - 1,)),
+        ],
+        compiler_params=pltpu.CompilerParams(vmem_limit_bytes=VMEM_ALL),
         cost_estimate=pl.CostEstimate(flops=1024, bytes_accessed=1024, transcendentals=0),
     )(x)
+
+
+def add_kernel(pieces, out_ref):
+    total = pieces[0]
+    for k in range(1, pieces.shape[0]):
+        total = total + pieces[k]
+    for k in range(pieces.shape[0]):
+        out_ref[k] = total
 
 
 def sum_over_rows(gram):
     count = lax.axis_size("row")
     pieces = gram.reshape(count, gram.shape[0] // count, gram.shape[1])
     theirs = lax.all_to_all(pieces, "row", 0, 0, tiled=True)
-    own = jnp.sum(theirs, axis=0)
-    spread = jnp.broadcast_to(own[None], pieces.shape)
+    spread = pl.pallas_call(
+        add_kernel,
+        out_shape=jax.ShapeDtypeStruct(pieces.shape, F32),
+        in_specs=[pl.BlockSpec(memory_space=pltpu.VMEM)],
+        out_specs=pl.BlockSpec(memory_space=pltpu.VMEM),
+        compiler_params=pltpu.CompilerParams(vmem_limit_bytes=8 * 2**20),
+        cost_estimate=pl.CostEstimate(flops=1024, bytes_accessed=1024, transcendentals=0),
+    )(theirs)
     return lax.all_to_all(spread, "row", 0, 0, tiled=True).reshape(gram.shape)
 
 
 def transform_kernel(swap_ref, gram_ref, inner_ref, outer_ref, work):
     n = work.shape[0]
     half = n // 2
-    work[:half, :half] = gram_ref[:half]
-    work[:half, half:] = gram_ref[half : 2 * half]
-    work[half:, :half] = gram_ref[half : 2 * half].T
-    work[half:, half:] = gram_ref[2 * half :]
+    for k, (i, j) in enumerate(UPPER):
+        block = gram_ref[k * LEAF : (k + 1) * LEAF]
+        work[i * LEAF : (i + 1) * LEAF, j * LEAF : (j + 1) * LEAF] = block
+        if i != j:
+            work[j * LEAF : (j + 1) * LEAF, i * LEAF : (i + 1) * LEAF] = block.T
 
     def block_step(p, carry):
         at = pl.ds(pl.multiple_of(p * LEAF, LEAF), LEAF)
@@ -175,7 +202,7 @@
 
 
 def make_transform(gram, swap):
-    n = 2 * gram.shape[1]
+    n = BLOCKS * LEAF
     return pl.pallas_call(
         transform_kernel,
         out_shape=[jax.ShapeDtypeStruct((n, n // 2), F32)] * 2,
@@ -187,6 +214,10 @@
     )(swap, gram)
 
 
+def tile_for(*extents):
+    return 512 if all(e % 512 == 0 for e in extents) else 256
+
+
 def apply_kernel(x_ref, t_inner, t_outer, inner_ref, outer_ref, parts):
     half = inner_ref.shape[1]
 
@@ -202,7 +233,8 @@
     outer_ref[...] = both[:, half:]
 
 
-def apply_rows(x, begin, rows, turns, tile=512):
+def apply_rows(x, begin, rows, turns):
+    tile = tile_for(begin, rows)
     n = x.shape[1]
     half = n // 2
     first = begin // tile
@@ -222,26 +254,30 @@
     )(x, *turns)
 
 
-def arrived_kernel(core_ref, inner, outer, t_inner, t_outer, *rest):
-    out, parts = rest[-2], rest[-1]
+def arrived_kernel(place_ref, inner, outer, t_inner, *rest):
+    t_outer, out, parts = rest[:PIECES], rest[-2], rest[-1]
     half = t_inner.shape[1]
+    piece = t_inner.shape[0] // PIECES
 
     @pl.when(pl.program_id(0) == 0)
     def _():
-        for side, t in enumerate((t_inner, t_outer)):
+        parts[0, 0], parts[0, 1] = split(t_inner[...])
+        for d, t in enumerate(t_outer):
+            at = pl.ds(pl.multiple_of((place_ref[1] + PIECES - d) % PIECES * piece, piece), piece)
             hi, lo = split(t[...])
-            parts[side, 0] = hi
-            parts[side, 1] = lo
+            parts[1, 0, at] = hi
+            parts[1, 1, at] = lo
 
     for side, block in enumerate((inner, outer)):
-        at = pl.ds(pl.multiple_of(jnp.bitwise_xor(core_ref[0], 1 - side) * half, half), half)
+        at = pl.ds(pl.multiple_of(jnp.bitwise_xor(place_ref[0], 1 - side) * half, half), half)
         out[:, at] = dot3(split(block[...]), (parts[side, 0], parts[side, 1]))
 
 
-def arrived_rows(out, shape, begin, rows, core, blocks, skip, turns, tile=512):
+def arrived_rows(out, shape, begin, rows, place, blocks, skip, turns):
     n = shape[1]
+    tile = tile_for(begin, rows, skip)
     first, here = begin // tile, skip // tile
-    args = [core, *blocks, *turns] + ([] if out is None else [out])
+    args = [place, *blocks, *turns] + ([] if out is None else [out])
     return pl.pallas_call(
         arrived_kernel,
         grid=(rows // tile,),
@@ -249,10 +285,9 @@
             pl.BlockSpec(memory_space=pltpu.SMEM),
             pl.BlockSpec((tile, n), lambda i: (here + i, 0)),
             pl.BlockSpec((tile, n), lambda i: (here + i, 0)),
-            pl.BlockSpec((n, n // 2), lambda i: (0, 0)),
-            pl.BlockSpec((n, n // 2), lambda i: (0, 0)),
         ]
-        + [pl.BlockSpec(memory_space=pl.ANY)] * (len(args) - 5),
+        + [pl.BlockSpec(t.shape, lambda i: (0, 0)) for t in turns]
+        + [pl.BlockSpec(memory_space=pl.ANY)] * (out is not None),
         out_specs=pl.BlockSpec((tile, n), lambda i: (first + i, 0)),
         scratch_shapes=[pltpu.VMEM((2, 2, n, n // 2), BF16)],
         out_shape=jax.ShapeDtypeStruct(shape, F32),
@@ -270,8 +305,9 @@
         out[:, at] = block[...]
 
 
-def place_rows(out, shape, begin, core, blocks, tile=512):
+def place_rows(out, shape, begin, core, blocks):
     rows, half = blocks[0].shape
+    tile = tile_for(begin, rows)
     first = begin // tile
     args = [core, *blocks] + ([] if out is None else [out])
     return pl.pallas_call(
@@ -311,23 +347,37 @@
     def pass_on(inner, outer):
         return lax.ppermute(inner, "col", within), lax.ppermute(outer, "col", across)
 
+    count_row = lax.axis_size("row")
+    ring = lax.axis_index("row") // (count_row // PIECES)
+    place = jnp.concatenate([core, jnp.reshape(ring, (1,)).astype(jnp.int32)])
+
     gram = sum_over_rows(make_gram(matrix))
     raw, gram = lax.optimization_barrier((raw_rows(sources), gram))
     early = pass_on(raw, raw)
     own_turns = make_transform(gram, swap)
-    waits = [early, pass_on(*own_turns)]
-    for which, begin, rows in LATE:
-        blocks = apply_rows(sources[which], begin, rows, own_turns)
-        blocks, waits[-2] = lax.optimization_barrier((blocks, waits[-2]))
-        waits.append(pass_on(*blocks))
-    early, turns = waits[:2]
+    piece = own_turns[1].shape[0] // PIECES
+    t_inner = lax.ppermute(own_turns[0], "col", within)
+    t_piece = lax.ppermute(lax.dynamic_slice_in_dim(own_turns[1], ring * piece, piece), "col", across)
+    pieces, late = [t_piece], []
+    for k, (which, begin, rows) in enumerate(LATE):
+        inner, outer = apply_rows(sources[which], begin, rows, own_turns)
+        if k < DEPTH:
+            outer, pieces[0], early = lax.optimization_barrier((outer, pieces[0], early))
+        else:
+            outer, late[k - DEPTH][1] = lax.optimization_barrier((outer, late[k - DEPTH][1]))
+        late.append(list(pass_on(inner, outer)))
+    for d in range(1, PIECES):
+        step = d * (count_row // PIECES)
+        around = [(i, (i + step) % count_row) for i in range(count_row)]
+        pieces.append(lax.ppermute(pieces[0], "row", around))
+    turns = (t_inner, *pieces)
     skip = 0
     for which, begin, rows in EARLY:
         results[which] = arrived_rows(
-            results[which], sources[which].shape, begin, rows, core, early, skip, turns
+            results[which], sources[which].shape, begin, rows, place, early, skip, turns
         )
         skip += rows
-    for (which, begin, rows), blocks in zip(LATE, waits[2:]):
+    for (which, begin, rows), blocks in zip(LATE, late):
         results[which] = place_rows(results[which], sources[which].shape, begin, core, blocks)
     return tuple(results)
 

time: 186 us -> 179 us (0.962)
  waiting for transfers between devices: 59.8 us -> 50.3 us
  starting transfers between devices: 27.6 us -> 32.5 us
  local copies, waits for them, and re-layouts: 6.22 us -> 3.1 us
  Pallas kernels: 60.4 us -> 62.9 us
  blocking collectives: 31 us -> 28.6 us
    ppermute x6 -> x5, waiting for transfers between devices: 59.8 us -> 40.4 us  [pass_on(): lax.ppermute(outer, 'col', across)]
    ppermute x0 -> x5, waiting for transfers between devices: none -> 9.8 us  [the longest x3 7.72 us: on_device(): pieces.append(lax.ppermute(pieces[0], 'row', around))]
    ppermute x0 -> x5, starting transfers between devices: none -> 5.43 us  [the longest x1 3.56 us: on_device(): lax.ppermute(lax.dynamic_slice_in_dim(own_turns[1], ring * piece, piece),...]
    unnamed x4 -> x2, local copies, waits for them, and re-layouts: 6.16 us -> 3.08 us
    pallas_call x1 -> x2, Pallas kernels: 5.31 us -> 7.76 us  [the longest x1 7.7 us: make_gram(): pl.pallas_call(functools.partial(gram_kernel, cuts), out_shape=jax.ShapeD...]
    ppermute x6 -> x5, starting transfers between devices: 26.2 us -> 26.1 us  [pass_on(): lax.ppermute(outer, 'col', across)]
  transfers between devices with their start and end apart: 12 -> 15, of which waited for: 5 -> 6; matrix products, arithmetic and copies ran while one was open for 0% -> 0% of each run, Pallas kernels for 29% -> 30%
where the time goes in v3:
time: 179 us; the launch traced here: 178 us
  Pallas kernels  62.9 us (35%)
  waiting for transfers between devices  50.3 us (28%)
  starting transfers between devices  32.5 us (18%)
  blocking collectives  28.6 us (16%)
  local copies, waits for them, and re-layouts  3.1 us (2%)
    ppermute x5, waiting for transfers between devices, pass_on(): lax.ppermute(outer, 'col', across)  40.4 us
    pallas_call x1, Pallas kernels, make_transform(): pl.pallas_call(transform_kernel, out_shape=[jax.ShapeDtypeStruct((n, n //...  38 us
    ppermute x5, starting transfers between devices, pass_on(): lax.ppermute(outer, 'col', across)  26.1 us
    all_to_all x1, blocking collectives, sum_over_rows(): theirs = lax.all_to_all(pieces, 'row', 0, 0, tiled=True)  16.7 us
    all_to_all x1, blocking collectives, sum_over_rows(): return lax.all_to_all(spread, 'row', 0, 0, tiled=True).reshape(gram.shape)  11.9 us
    ppermute x3, waiting for transfers between devices, on_device(): pieces.append(lax.ppermute(pieces[0], 'row', around))  7.72 us
    pallas_call x1, Pallas kernels, make_gram(): pl.pallas_call(functools.partial(gram_kernel, cuts), out_shape=jax.ShapeD...  7.7 us
    pallas_call x4, Pallas kernels, apply_rows(): pl.pallas_call(apply_kernel, grid=(rows // tile,), out_shape=[jax.ShapeDt...  7.49 us
  transfers between devices with their start and end apart: 15, of which 6 were waited for; matrix products, arithmetic and copies ran while one was open for 0% of the time, Pallas kernels for 30%

profile of v3, /device:TPU:3, one launch (start us, length us, event | category | flops | bytes accessed | tf_op | source)
XLA Modules:
  0.0 178.3 jit_solution(9029969888156332865)
XLA Ops:
  0.6 7.7 %shard_map.41 = f32[1280,128]{1,0:T(8,128)} custom-call(f32[3584,512]{1,0:T(8,128)} %x_ref.7), custom_call_target="tpu_custom_call" | custom-call | flops 1024 | bytes 1024 | tf_op jit(solution)/shard_map/pallas_call | solution.py:114
  8.3 16.7 %all_to_all.10.pieces = f32[8,160,128]{2,1,0:T(8,128)S(1)} all-to-all(f32[8,160,128]{2,1,0:T(8,128)} %bitcast.6), channel_id=1, replica_groups=mesh['col'=16,'row'=8] {'row'}, dimensions={0} | all-to-all | bytes 1310720 | tf_op jit(solution)/shard_map/all_to_all | solution.py:141
  25.1 11.9 %all_to_all.11 = f32[8,160,128]{2,1,0:T(8,128)S(1)} all-to-all(f32[8,160,128]{2,1,0:T(8,128)S(1)} %shard_map.42), channel_id=1, replica_groups=mesh['col'=16,'row'=8] {'row'}, dimensions={0} | all-to-all | bytes 1310720 | tf_op jit(solution)/shard_map/all_to_all | solution.py:150
  37.0 7.4 %collective-permute-start.3 = (f32[1024,512]{1,0:T(8,128)}, f32[1024,512]{1,0:T(8,128)S(1)}, u32[]{:S(2)}, u32[]{:S(2)}) collective-permute-start(f32[1024,512]{1,0:T(8,128)} %param.3), channel_id=1, source_target_pairs={{0,0},{120,120},{8,16},{24,32},{40,48},{56,64},{72,80},{88,96},{10... | collective-permute-start | bytes 6291464 | tf_op jit(solution)/shard_map/ppermute | solution.py:348
  44.7 38.0 %shard_map.43 = (f32[512,256]{1,0:T(8,128)S(1)}, f32[512,256]{1,0:T(8,128)S(1)}) custom-call(s32[1]{0:T(128)S(6)} %select_n.24.swap_ref, f32[1280,128]{1,0:T(8,128)S(1)} %bitcast.5), custom_call_target="tpu_custom_call" | custom-call | flops 1024 | bytes 1024 | tf_op jit(solution)/shard_map/pallas_call | solution.py:206
  82.7 3.6 %collective-permute-start.1 = (f32[128,256]{1,0:T(8,128)S(1)}, f32[128,256]{1,0:T(8,128)S(1)}, u32[]{:S(2)}, u32[]{:S(2)}) collective-permute-start(f32[128,256]{1,0:T(8,128)S(1)} %constant_dynamic-slice_fusion), channel_id=1, source_target_pairs={{0,0},{120,120},{8,16},{24,32},{40,48},{56,64},{72,80},{88,96},{10... | collective-permute-start | bytes 393224 | tf_op jit(solution)/shard_map/ppermute | solution.py:360
  86.3 3.1 %copy-done = f32[3584,512]{1,0:T(8,128)S(1)} copy-done((f32[3584,512]{1,0:T(8,128)S(1)}, f32[3584,512]{1,0:T(8,128)}, u32[]{:S(2)}) %copy-start) | copy-done | bytes 7340056
  89.4 2.2 %shard_map.46 = (f32[1024,256]{1,0:T(8,128)S(1)}, f32[1024,256]{1,0:T(8,128)S(1)}) custom-call(f32[3584,512]{1,0:T(8,128)S(1)} %copy-done, f32[512,256]{1,0:T(8,128)S(1)} %get-tuple-element.27.t_inner, f32[512,256]{1,0:T(8,128)S(1)} %get-tuple-element.28.t_outer), custom_call_target="tpu_custom_call" | custom-call | flops 1610612736 | bytes 4194304 | tf_op jit(solution)/shard_map/pallas_call | solution.py:241
  91.5 2.1 %collective-permute-done.1.rest_0_ = f32[128,256]{1,0:T(8,128)S(1)} collective-permute-done((f32[128,256]{1,0:T(8,128)S(1)}, f32[128,256]{1,0:T(8,128)S(1)}, u32[]{:S(2)}, u32[]{:S(2)}) %collective-permute-start.1) | collective-permute-done | bytes 131104 | tf_op jit(solution)/shard_map/ppermute | solution.py:360
  93.6 3.8 %collective-permute-start.7 = (f32[1024,256]{1,0:T(8,128)S(1)}, f32[1024,256]{1,0:T(8,128)S(1)}, u32[]{:S(2)}, u32[]{:S(2)}) collective-permute-start(f32[1024,256]{1,0:T(8,128)S(1)} %get-tuple-element.41), channel_id=1, source_target_pairs={{0,0},{120,120},{8,16},{24,32},{40,48},{56,64},{72,80},{88,96},{10... | collective-permute-start | bytes 3145736 | tf_op jit(solution)/shard_map/ppermute | solution.py:348
  97.5 2.2 %shard_map.45 = (f32[1024,256]{1,0:T(8,128)S(1)}, f32[1024,256]{1,0:T(8,128)S(1)}) custom-call(f32[3584,512]{1,0:T(8,128)S(1)} %copy-done, f32[512,256]{1,0:T(8,128)S(1)} %get-tuple-element.27.t_inner, f32[512,256]{1,0:T(8,128)S(1)} %get-tuple-element.28.t_outer), custom_call_target="tpu_custom_call" | custom-call | flops 1610612736 | bytes 4194304 | tf_op jit(solution)/shard_map/pallas_call | solution.py:241
  99.7 3.3 %collective-permute-start.4 = (f32[1024,256]{1,0:T(8,128)S(1)}, f32[1024,256]{1,0:T(8,128)S(1)}, u32[]{:S(2)}, u32[]{:S(2)}) collective-permute-start(f32[1024,256]{1,0:T(8,128)S(1)} %get-tuple-element.37), channel_id=1, source_target_pairs={{0,0},{120,120},{8,16},{24,32},{40,48},{56,64},{72,80},{88,96},{10... | collective-permute-start | bytes 3145736 | tf_op jit(solution)/shard_map/ppermute | solution.py:348
  103.1 2.2 %shard_map.47 = (f32[1024,256]{1,0:T(8,128)S(1)}, f32[1024,256]{1,0:T(8,128)S(1)}) custom-call(f32[3584,512]{1,0:T(8,128)S(1)} %copy-done, f32[512,256]{1,0:T(8,128)S(1)} %get-tuple-element.27.t_inner, f32[512,256]{1,0:T(8,128)S(1)} %get-tuple-element.28.t_outer), custom_call_target="tpu_custom_call" | custom-call | flops 1610612736 | bytes 4194304 | tf_op jit(solution)/shard_map/pallas_call | solution.py:241
  105.8 26.5 %collective-permute-done.7.outer = f32[1024,256]{1,0:T(8,128)S(1)} collective-permute-done((f32[1024,256]{1,0:T(8,128)S(1)}, f32[1024,256]{1,0:T(8,128)S(1)}, u32[]{:S(2)}, u32[]{:S(2)}) %collective-permute-start.7) | collective-permute-done | bytes 1048608 | tf_op jit(solution)/shard_map/ppermute | solution.py:348
  132.3 5.2 %collective-permute-start.8 = (f32[1024,256]{1,0:T(8,128)S(1)}, f32[1024,256]{1,0:T(8,128)S(1)}, u32[]{:S(2)}, u32[]{:S(2)}) collective-permute-start(f32[1024,256]{1,0:T(8,128)S(1)} %get-tuple-element.42), channel_id=1, source_target_pairs={{0,0},{120,120},{8,16},{24,32},{40,48},{56,64},{72,80},{88,96},{10... | collective-permute-start | bytes 3145736 | tf_op jit(solution)/shard_map/ppermute | solution.py:348
  138.3 3.9 %collective-permute-done.14.rest_3_ = f32[128,256]{1,0:T(8,128)S(1)} collective-permute-done((f32[128,256]{1,0:T(8,128)S(1)}, f32[128,256]{1,0:T(8,128)S(1)}, u32[]{:S(2)}, u32[]{:S(2)}) %collective-permute-start.14) | collective-permute-done | bytes 131104 | tf_op jit(solution)/shard_map/ppermute | solution.py:372
  143.1 11.7 %collective-permute-done.4.outer = f32[1024,256]{1,0:T(8,128)S(1)} collective-permute-done((f32[1024,256]{1,0:T(8,128)S(1)}, f32[1024,256]{1,0:T(8,128)S(1)}, u32[]{:S(2)}, u32[]{:S(2)}) %collective-permute-start.4) | collective-permute-done | bytes 1048608 | tf_op jit(solution)/shard_map/ppermute | solution.py:348
  155.9 3.8 %collective-permute-done.12.rest_1_ = f32[128,256]{1,0:T(8,128)S(1)} collective-permute-done((f32[128,256]{1,0:T(8,128)S(1)}, f32[128,256]{1,0:T(8,128)S(1)}, u32[]{:S(2)}, u32[]{:S(2)}) %collective-permute-start.12) | collective-permute-done | bytes 131104 | tf_op jit(solution)/shard_map/ppermute | solution.py:372
  159.8 6.4 %collective-permute-start.5 = (f32[512,256]{1,0:T(8,128)S(1)}, f32[512,256]{1,0:T(8,128)S(1)}, u32[]{:S(2)}, u32[]{:S(2)}) collective-permute-start(f32[512,256]{1,0:T(8,128)S(1)} %get-tuple-element.38), channel_id=1, source_target_pairs={{0,0},{120,120},{8,16},{24,32},{40,48},{56,64},{72,80},{88,96},{10... | collective-permute-start | bytes 1572872 | tf_op jit(solution)/shard_map/ppermute | solution.py:348
  166.2 4.4 %shard_map.52 = f32[1024,512]{1,0:T(8,128)} custom-call(s32[2]{0:T(128)S(1)} %pad_add_fusion.place_ref, f32[1024,512]{1,0:T(8,128)} %collective-permute-done.2.inner, f32[1024,512]{1,0:T(8,128)S(1)} %collective-permute-done.3.outer, f32[512,256]{1,0:T(8,128)S(1)} %collective-permute-done.11.t_inner, f32[128,256]{1,0:T(8,128)S(1)} %collective-permute-done.1.rest_0_, ...), custom_call_target="tpu_custom_call" | custom-call | flops 1610612736 | bytes 4194304 | tf_op jit(solution)/shard_map/pallas_call | solution.py:281
  170.7 1.4 shard_map.48.rest_0_
  172.1 1.4 shard_map.49.rest_0_
  173.5 1.4 shard_map.50.rest_0_
  174.9 2.3 %collective-permute-done.5.outer = f32[512,256]{1,0:T(8,128)S(1)} collective-permute-done((f32[512,256]{1,0:T(8,128)S(1)}, f32[512,256]{1,0:T(8,128)S(1)}, u32[]{:S(2)}, u32[]{:S(2)}) %collective-permute-start.5) | collective-permute-done | bytes 524320 | tf_op jit(solution)/shard_map/ppermute | solution.py:348
  (24 shorter events, 5.1 us)
Async XLA Ops:
  37.0 56.6 %collective-permute-start.3 = (f32[1024,512]{1,0:T(8,128)}, f32[1024,512]{1,0:T(8,128)S(1)}, u32[]{:S(2)}, u32[]{:S(2)}) collective-permute-start(f32[1024,512]{1,0:T(8,128)} %param.3), channel_id=1, source_target_pairs={{0,0},{120,120},{8,16},{24,32},{40,48},{56,64},{72,80},{88,96},{10... | collective-permute-start | bytes 6291464 | tf_op jit(solution)/shard_map/ppermute | solution.py:348
  44.4 49.2 %collective-permute-start.2 = (f32[1024,512]{1,0:T(8,128)}, f32[1024,512]{1,0:T(8,128)}, u32[]{:S(2)}, u32[]{:S(2)}) collective-permute-start(f32[1024,512]{1,0:T(8,128)} %param.3), channel_id=1, source_target_pairs={{0,8},{8,0},{16,24},{24,16},{32,40},{40,32},{48,56},{56,48},{64,72... | collective-permute-start | bytes 6291464 | tf_op jit(solution)/shard_map/ppermute | solution.py:348
  82.7 10.9 %collective-permute-start.1 = (f32[128,256]{1,0:T(8,128)S(1)}, f32[128,256]{1,0:T(8,128)S(1)}, u32[]{:S(2)}, u32[]{:S(2)}) collective-permute-start(f32[128,256]{1,0:T(8,128)S(1)} %constant_dynamic-slice_fusion), channel_id=1, source_target_pairs={{0,0},{120,120},{8,16},{24,32},{40,48},{56,64},{72,80},{88,96},{10... | collective-permute-start | bytes 393224 | tf_op jit(solution)/shard_map/ppermute | solution.py:360
  86.3 3.1 %copy-start = (f32[3584,512]{1,0:T(8,128)S(1)}, f32[3584,512]{1,0:T(8,128)}, u32[]{:S(2)}) copy-start(f32[3584,512]{1,0:T(8,128)} %x_ref.7) | copy-start | bytes 22020100
  93.6 38.6 %collective-permute-start.7 = (f32[1024,256]{1,0:T(8,128)S(1)}, f32[1024,256]{1,0:T(8,128)S(1)}, u32[]{:S(2)}, u32[]{:S(2)}) collective-permute-start(f32[1024,256]{1,0:T(8,128)S(1)} %get-tuple-element.41), channel_id=1, source_target_pairs={{0,0},{120,120},{8,16},{24,32},{40,48},{56,64},{72,80},{88,96},{10... | collective-permute-start | bytes 3145736 | tf_op jit(solution)/shard_map/ppermute | solution.py:348
  97.4 40.1 %collective-permute-start.10 = (f32[1024,256]{1,0:T(8,128)S(1)}, f32[1024,256]{1,0:T(8,128)S(1)}, u32[]{:S(2)}, u32[]{:S(2)}) collective-permute-start(f32[1024,256]{1,0:T(8,128)S(1)} %get-tuple-element.45), channel_id=1, source_target_pairs={{0,8},{8,0},{16,24},{24,16},{32,40},{40,32},{48,56},{56,48},{64,72... | collective-permute-start | bytes 3145736 | tf_op jit(solution)/shard_map/ppermute | solution.py:348
  99.7 55.0 %collective-permute-start.4 = (f32[1024,256]{1,0:T(8,128)S(1)}, f32[1024,256]{1,0:T(8,128)S(1)}, u32[]{:S(2)}, u32[]{:S(2)}) collective-permute-start(f32[1024,256]{1,0:T(8,128)S(1)} %get-tuple-element.37), channel_id=1, source_target_pairs={{0,0},{120,120},{8,16},{24,32},{40,48},{56,64},{72,80},{88,96},{10... | collective-permute-start | bytes 3145736 | tf_op jit(solution)/shard_map/ppermute | solution.py:348
  103.0 29.3 %collective-permute-start.11 = (f32[512,256]{1,0:T(8,128)S(1)}, f32[512,256]{1,0:T(8,128)S(1)}, u32[]{:S(2)}, u32[]{:S(2)}) collective-permute-start(f32[512,256]{1,0:T(8,128)S(1)} %get-tuple-element.27.t_inner), channel_id=1, source_target_pairs={{0,8},{8,0},{16,24},{24,16},{32,40},{40,32},{48,56},{56,48},{64,72... | collective-permute-start | bytes 1572872 | tf_op jit(solution)/shard_map/ppermute | solution.py:359
  105.3 68.2 %collective-permute-start.6 = (f32[1024,256]{1,0:T(8,128)S(1)}, f32[1024,256]{1,0:T(8,128)S(1)}, u32[]{:S(2)}, u32[]{:S(2)}) collective-permute-start(f32[1024,256]{1,0:T(8,128)S(1)} %get-tuple-element.39), channel_id=1, source_target_pairs={{0,8},{8,0},{16,24},{24,16},{32,40},{40,32},{48,56},{56,48},{64,72... | collective-permute-start | bytes 3145736 | tf_op jit(solution)/shard_map/ppermute | solution.py:348
  132.3 39.8 %collective-permute-start.9 = (f32[1024,256]{1,0:T(8,128)S(1)}, f32[1024,256]{1,0:T(8,128)S(1)}, u32[]{:S(2)}, u32[]{:S(2)}) collective-permute-start(f32[1024,256]{1,0:T(8,128)S(1)} %get-tuple-element.43), channel_id=1, source_target_pairs={{0,8},{8,0},{16,24},{24,16},{32,40},{40,32},{48,56},{56,48},{64,72... | collective-permute-start | bytes 3145736 | tf_op jit(solution)/shard_map/ppermute | solution.py:348
  132.3 41.2 %collective-permute-start.8 = (f32[1024,256]{1,0:T(8,128)S(1)}, f32[1024,256]{1,0:T(8,128)S(1)}, u32[]{:S(2)}, u32[]{:S(2)}) collective-permute-start(f32[1024,256]{1,0:T(8,128)S(1)} %get-tuple-element.42), channel_id=1, source_target_pairs={{0,0},{120,120},{8,16},{24,32},{40,48},{56,64},{72,80},{88,96},{10... | collective-permute-start | bytes 3145736 | tf_op jit(solution)/shard_map/ppermute | solution.py:348
  137.5 4.7 %collective-permute-start.14 = (f32[128,256]{1,0:T(8,128)S(1)}, f32[128,256]{1,0:T(8,128)S(1)}, u32[]{:S(2)}, u32[]{:S(2)}) collective-permute-start(f32[128,256]{1,0:T(8,128)S(1)} %collective-permute-done.1.rest_0_), channel_id=1, source_target_pairs={{0,6},{1,7},{2,0},{3,1},{4,2},{5,3},{6,4},{7,5},{8,14},{9,15},{10,... | collective-permute-start | bytes 393224 | tf_op jit(solution)/shard_map/ppermute | solution.py:372
  142.2 13.7 %collective-permute-start.13 = (f32[128,256]{1,0:T(8,128)S(1)}, f32[128,256]{1,0:T(8,128)S(1)}, u32[]{:S(2)}, u32[]{:S(2)}) collective-permute-start(f32[128,256]{1,0:T(8,128)S(1)} %collective-permute-done.1.rest_0_), channel_id=1, source_target_pairs={{0,4},{1,5},{2,6},{3,7},{4,0},{5,1},{6,2},{7,3},{8,12},{9,13},{10,... | collective-permute-start | bytes 393224 | tf_op jit(solution)/shard_map/ppermute | solution.py:372
  154.7 5.0 %collective-permute-start.12 = (f32[128,256]{1,0:T(8,128)S(1)}, f32[128,256]{1,0:T(8,128)S(1)}, u32[]{:S(2)}, u32[]{:S(2)}) collective-permute-start(f32[128,256]{1,0:T(8,128)S(1)} %collective-permute-done.1.rest_0_), channel_id=1, source_target_pairs={{0,2},{1,3},{2,4},{3,5},{4,6},{5,7},{6,0},{7,1},{8,10},{9,11},{10,... | collective-permute-start | bytes 393224 | tf_op jit(solution)/shard_map/ppermute | solution.py:372
  155.8 19.0 %collective-permute-start = (f32[512,256]{1,0:T(8,128)S(1)}, f32[512,256]{1,0:T(8,128)S(1)}, u32[]{:S(2)}, u32[]{:S(2)}) collective-permute-start(f32[512,256]{1,0:T(8,128)S(1)} %get-tuple-element.29), channel_id=1, source_target_pairs={{0,8},{8,0},{16,24},{24,16},{32,40},{40,32},{48,56},{56,48},{64,72... | collective-permute-start | bytes 1572872 | tf_op jit(solution)/shard_map/ppermute | solution.py:348
  159.8 17.4 %collective-permute-start.5 = (f32[512,256]{1,0:T(8,128)S(1)}, f32[512,256]{1,0:T(8,128)S(1)}, u32[]{:S(2)}, u32[]{:S(2)}) collective-permute-start(f32[512,256]{1,0:T(8,128)S(1)} %get-tuple-element.38), channel_id=1, source_target_pairs={{0,0},{120,120},{8,16},{24,32},{40,48},{56,64},{72,80},{88,96},{10... | collective-permute-start | bytes 1572872 | tf_op jit(solution)/shard_map/ppermute | solution.py:348

commit v4 on v3

--- a/solution.py
+++ b/solution.py
@@ -150,7 +150,7 @@
     return lax.all_to_all(spread, "row", 0, 0, tiled=True).reshape(gram.shape)
 
 
-def transform_kernel(swap_ref, gram_ref, inner_ref, outer_ref, work):
+def transform_kernel(swap_ref, gram_ref, inner_ref, outer_ref, work, gram):
     n = work.shape[0]
     half = n // 2
     for k, (i, j) in enumerate(UPPER):
@@ -191,8 +191,13 @@
     def polar_step(k, carry):
         z = work[...]
         zs = split(z)
-        g = dot3(zs, zs, NT)
-        work[...] = 1.5 * z - 0.5 * dot3(split(g), zs)
+        top = tuple(part[:half] for part in zs)
+        low = tuple(part[half:] for part in zs)
+        upper = dot3(top, zs, NT)
+        gram[:half, :] = upper
+        gram[half:, :half] = upper[:, half:].T
+        gram[half:, half:] = dot3(low, low, NT)
+        work[...] = 1.5 * z - 0.5 * dot3(split(gram[...]), zs)
         return carry
 
     lax.fori_loop(0, POLAR_STEPS, polar_step, 0)
@@ -208,7 +213,7 @@
         out_shape=[jax.ShapeDtypeStruct((n, n // 2), F32)] * 2,
         in_specs=[pl.BlockSpec(memory_space=pltpu.SMEM), pl.BlockSpec(memory_space=pltpu.VMEM)],
         out_specs=[pl.BlockSpec(memory_space=pltpu.VMEM)] * 2,
-        scratch_shapes=[pltpu.VMEM((n, n), F32)],
+        scratch_shapes=[pltpu.VMEM((n, n), F32)] * 2,
         compiler_params=pltpu.CompilerParams(vmem_limit_bytes=16 * 2**20),
         cost_estimate=pl.CostEstimate(flops=1024, bytes_accessed=1024, transcendentals=0),
     )(swap, gram)

time: 179 us -> 181 us (1.011)
  Pallas kernels: 62.9 us -> 65 us
  starting transfers between devices: 32.5 us -> 30.4 us
  waiting for transfers between devices: 50.3 us -> 52.2 us
    ppermute x5, waiting for transfers between devices: 40.4 us -> 44 us  [pass_on(): lax.ppermute(outer, 'col', across)]
    ppermute x5, starting transfers between devices: 26.1 us -> 22.8 us  [pass_on(): lax.ppermute(outer, 'col', across)]
    pallas_call x1, Pallas kernels: 38 us -> 40.1 us  [make_transform(): pl.pallas_call(transform_kernel, out_shape=[jax.ShapeDtypeStruct((n, n //...]
  transfers between devices with their start and end apart: 15 -> 15, of which waited for: 6 -> 6; matrix products, arithmetic and copies ran while one was open for 0% -> 0% of each run, Pallas kernels for 30% -> 31%
where the time goes in v4:
time: 181 us; the launch traced here: 180 us
  Pallas kernels  65 us (36%)
  waiting for transfers between devices  52.2 us (29%)
  starting transfers between devices  30.4 us (17%)
  blocking collectives  28.6 us (16%)
  local copies, waits for them, and re-layouts  3.1 us (2%)
    ppermute x5, waiting for transfers between devices, pass_on(): lax.ppermute(outer, 'col', across)  44 us
    pallas_call x1, Pallas kernels, make_transform(): pl.pallas_call(transform_kernel, out_shape=[jax.ShapeDtypeStruct((n, n //...  40.1 us
    ppermute x5, starting transfers between devices, pass_on(): lax.ppermute(outer, 'col', across)  22.8 us
    all_to_all x1, blocking collectives, sum_over_rows(): theirs = lax.all_to_all(pieces, 'row', 0, 0, tiled=True)  16.7 us
    all_to_all x1, blocking collectives, sum_over_rows(): return lax.all_to_all(spread, 'row', 0, 0, tiled=True).reshape(gram.shape)  11.9 us
    ppermute x3, waiting for transfers between devices, on_device(): pieces.append(lax.ppermute(pieces[0], 'row', around))  7.73 us
    pallas_call x1, Pallas kernels, make_gram(): pl.pallas_call(functools.partial(gram_kernel, cuts), out_shape=jax.ShapeD...  7.7 us
    pallas_call x4, Pallas kernels, apply_rows(): pl.pallas_call(apply_kernel, grid=(rows // tile,), out_shape=[jax.ShapeDt...  7.47 us
  transfers between devices with their start and end apart: 15, of which 6 were waited for; matrix products, arithmetic and copies ran while one was open for 0% of the time, Pallas kernels for 31%

profile of v4, /device:TPU:3, one launch (start us, length us, event | category | flops | bytes accessed | tf_op | source)
XLA Modules:
  0.0 180.1 jit_solution(2095368854599925900)
XLA Ops:
  0.6 7.7 %shard_map.41 = f32[1280,128]{1,0:T(8,128)} custom-call(f32[3584,512]{1,0:T(8,128)} %x_ref.7), custom_call_target="tpu_custom_call" | custom-call | flops 1024 | bytes 1024 | tf_op jit(solution)/shard_map/pallas_call | solution.py:114
  8.3 16.7 %all_to_all.10.pieces = f32[8,160,128]{2,1,0:T(8,128)S(1)} all-to-all(f32[8,160,128]{2,1,0:T(8,128)} %bitcast.6), channel_id=1, replica_groups=mesh['col'=16,'row'=8] {'row'}, dimensions={0} | all-to-all | bytes 1310720 | tf_op jit(solution)/shard_map/all_to_all | solution.py:141
  25.1 11.9 %all_to_all.11 = f32[8,160,128]{2,1,0:T(8,128)S(1)} all-to-all(f32[8,160,128]{2,1,0:T(8,128)S(1)} %shard_map.42), channel_id=1, replica_groups=mesh['col'=16,'row'=8] {'row'}, dimensions={0} | all-to-all | bytes 1310720 | tf_op jit(solution)/shard_map/all_to_all | solution.py:150
  37.0 7.4 %collective-permute-start.3 = (f32[1024,512]{1,0:T(8,128)}, f32[1024,512]{1,0:T(8,128)S(1)}, u32[]{:S(2)}, u32[]{:S(2)}) collective-permute-start(f32[1024,512]{1,0:T(8,128)} %param.3), channel_id=1, source_target_pairs={{0,0},{120,120},{8,16},{24,32},{40,48},{56,64},{72,80},{88,96},{10... | collective-permute-start | bytes 6291464 | tf_op jit(solution)/shard_map/ppermute | solution.py:353
  44.7 40.1 %shard_map.43 = (f32[512,256]{1,0:T(8,128)S(1)}, f32[512,256]{1,0:T(8,128)S(1)}) custom-call(s32[1]{0:T(128)S(6)} %select_n.24.swap_ref, f32[1280,128]{1,0:T(8,128)S(1)} %bitcast.5), custom_call_target="tpu_custom_call" | custom-call | flops 1024 | bytes 1024 | tf_op jit(solution)/shard_map/pallas_call | solution.py:211
  84.8 3.6 %collective-permute-start.1 = (f32[128,256]{1,0:T(8,128)S(1)}, f32[128,256]{1,0:T(8,128)S(1)}, u32[]{:S(2)}, u32[]{:S(2)}) collective-permute-start(f32[128,256]{1,0:T(8,128)S(1)} %constant_dynamic-slice_fusion), channel_id=1, source_target_pairs={{0,0},{120,120},{8,16},{24,32},{40,48},{56,64},{72,80},{88,96},{10... | collective-permute-start | bytes 393224 | tf_op jit(solution)/shard_map/ppermute | solution.py:365
  88.4 3.1 %copy-done = f32[3584,512]{1,0:T(8,128)S(1)} copy-done((f32[3584,512]{1,0:T(8,128)S(1)}, f32[3584,512]{1,0:T(8,128)}, u32[]{:S(2)}) %copy-start) | copy-done | bytes 7340056
  91.5 2.2 %shard_map.46 = (f32[1024,256]{1,0:T(8,128)S(1)}, f32[1024,256]{1,0:T(8,128)S(1)}) custom-call(f32[3584,512]{1,0:T(8,128)S(1)} %copy-done, f32[512,256]{1,0:T(8,128)S(1)} %get-tuple-element.27.t_inner, f32[512,256]{1,0:T(8,128)S(1)} %get-tuple-element.28.t_outer), custom_call_target="tpu_custom_call" | custom-call | flops 1610612736 | bytes 4194304 | tf_op jit(solution)/shard_map/pallas_call | solution.py:246
  94.0 3.6 %collective-permute-start.7 = (f32[1024,256]{1,0:T(8,128)S(1)}, f32[1024,256]{1,0:T(8,128)S(1)}, u32[]{:S(2)}, u32[]{:S(2)}) collective-permute-start(f32[1024,256]{1,0:T(8,128)S(1)} %get-tuple-element.41), channel_id=1, source_target_pairs={{0,0},{120,120},{8,16},{24,32},{40,48},{56,64},{72,80},{88,96},{10... | collective-permute-start | bytes 3145736 | tf_op jit(solution)/shard_map/ppermute | solution.py:353
  98.6 2.2 %shard_map.45 = (f32[1024,256]{1,0:T(8,128)S(1)}, f32[1024,256]{1,0:T(8,128)S(1)}) custom-call(f32[3584,512]{1,0:T(8,128)S(1)} %copy-done, f32[512,256]{1,0:T(8,128)S(1)} %get-tuple-element.27.t_inner, f32[512,256]{1,0:T(8,128)S(1)} %get-tuple-element.28.t_outer), custom_call_target="tpu_custom_call" | custom-call | flops 1610612736 | bytes 4194304 | tf_op jit(solution)/shard_map/pallas_call | solution.py:246
  100.8 3.5 %collective-permute-start.4 = (f32[1024,256]{1,0:T(8,128)S(1)}, f32[1024,256]{1,0:T(8,128)S(1)}, u32[]{:S(2)}, u32[]{:S(2)}) collective-permute-start(f32[1024,256]{1,0:T(8,128)S(1)} %get-tuple-element.37), channel_id=1, source_target_pairs={{0,0},{120,120},{8,16},{24,32},{40,48},{56,64},{72,80},{88,96},{10... | collective-permute-start | bytes 3145736 | tf_op jit(solution)/shard_map/ppermute | solution.py:353
  104.4 2.2 %shard_map.47 = (f32[1024,256]{1,0:T(8,128)S(1)}, f32[1024,256]{1,0:T(8,128)S(1)}) custom-call(f32[3584,512]{1,0:T(8,128)S(1)} %copy-done, f32[512,256]{1,0:T(8,128)S(1)} %get-tuple-element.27.t_inner, f32[512,256]{1,0:T(8,128)S(1)} %get-tuple-element.28.t_outer), custom_call_target="tpu_custom_call" | custom-call | flops 1610612736 | bytes 4194304 | tf_op jit(solution)/shard_map/pallas_call | solution.py:246
  107.2 26.9 %collective-permute-done.7.outer = f32[1024,256]{1,0:T(8,128)S(1)} collective-permute-done((f32[1024,256]{1,0:T(8,128)S(1)}, f32[1024,256]{1,0:T(8,128)S(1)}, u32[]{:S(2)}, u32[]{:S(2)}) %collective-permute-start.7) | collective-permute-done | bytes 1048608 | tf_op jit(solution)/shard_map/ppermute | solution.py:353
  134.1 3.6 %collective-permute-start.8 = (f32[1024,256]{1,0:T(8,128)S(1)}, f32[1024,256]{1,0:T(8,128)S(1)}, u32[]{:S(2)}, u32[]{:S(2)}) collective-permute-start(f32[1024,256]{1,0:T(8,128)S(1)} %get-tuple-element.42), channel_id=1, source_target_pairs={{0,0},{120,120},{8,16},{24,32},{40,48},{56,64},{72,80},{88,96},{10... | collective-permute-start | bytes 3145736 | tf_op jit(solution)/shard_map/ppermute | solution.py:353
  138.7 3.9 %collective-permute-done.14.rest_3_ = f32[128,256]{1,0:T(8,128)S(1)} collective-permute-done((f32[128,256]{1,0:T(8,128)S(1)}, f32[128,256]{1,0:T(8,128)S(1)}, u32[]{:S(2)}, u32[]{:S(2)}) %collective-permute-start.14) | collective-permute-done | bytes 131104 | tf_op jit(solution)/shard_map/ppermute | solution.py:377
  143.5 13.1 %collective-permute-done.4.outer = f32[1024,256]{1,0:T(8,128)S(1)} collective-permute-done((f32[1024,256]{1,0:T(8,128)S(1)}, f32[1024,256]{1,0:T(8,128)S(1)}, u32[]{:S(2)}, u32[]{:S(2)}) %collective-permute-start.4) | collective-permute-done | bytes 1048608 | tf_op jit(solution)/shard_map/ppermute | solution.py:353
  157.8 3.8 %collective-permute-done.12.rest_1_ = f32[128,256]{1,0:T(8,128)S(1)} collective-permute-done((f32[128,256]{1,0:T(8,128)S(1)}, f32[128,256]{1,0:T(8,128)S(1)}, u32[]{:S(2)}, u32[]{:S(2)}) %collective-permute-start.12) | collective-permute-done | bytes 131104 | tf_op jit(solution)/shard_map/ppermute | solution.py:377
  161.6 4.7 %collective-permute-start.5 = (f32[512,256]{1,0:T(8,128)S(1)}, f32[512,256]{1,0:T(8,128)S(1)}, u32[]{:S(2)}, u32[]{:S(2)}) collective-permute-start(f32[512,256]{1,0:T(8,128)S(1)} %get-tuple-element.38), channel_id=1, source_target_pairs={{0,0},{120,120},{8,16},{24,32},{40,48},{56,64},{72,80},{88,96},{10... | collective-permute-start | bytes 1572872 | tf_op jit(solution)/shard_map/ppermute | solution.py:353
  166.4 4.4 %shard_map.52 = f32[1024,512]{1,0:T(8,128)} custom-call(s32[2]{0:T(128)S(1)} %pad_add_fusion.place_ref, f32[1024,512]{1,0:T(8,128)} %collective-permute-done.2.inner, f32[1024,512]{1,0:T(8,128)S(1)} %collective-permute-done.3.outer, f32[512,256]{1,0:T(8,128)S(1)} %collective-permute-done.11.t_inner, f32[128,256]{1,0:T(8,128)S(1)} %collective-permute-done.1.rest_0_, ...), custom_call_target="tpu_custom_call" | custom-call | flops 1610612736 | bytes 4194304 | tf_op jit(solution)/shard_map/pallas_call | solution.py:286
  170.8 1.4 shard_map.48.rest_0_
  172.2 1.4 shard_map.49.rest_0_
  173.6 1.4 shard_map.50.rest_0_
  175.1 4.0 %collective-permute-done.5.outer = f32[512,256]{1,0:T(8,128)S(1)} collective-permute-done((f32[512,256]{1,0:T(8,128)S(1)}, f32[512,256]{1,0:T(8,128)S(1)}, u32[]{:S(2)}, u32[]{:S(2)}) %collective-permute-start.5) | collective-permute-done | bytes 524320 | tf_op jit(solution)/shard_map/ppermute | solution.py:353
  179.0 1.1 shard_map.51
  (24 shorter events, 5.6 us)
Async XLA Ops:
  37.0 57.0 %collective-permute-start.3 = (f32[1024,512]{1,0:T(8,128)}, f32[1024,512]{1,0:T(8,128)S(1)}, u32[]{:S(2)}, u32[]{:S(2)}) collective-permute-start(f32[1024,512]{1,0:T(8,128)} %param.3), channel_id=1, source_target_pairs={{0,0},{120,120},{8,16},{24,32},{40,48},{56,64},{72,80},{88,96},{10... | collective-permute-start | bytes 6291464 | tf_op jit(solution)/shard_map/ppermute | solution.py:353
  44.4 49.6 %collective-permute-start.2 = (f32[1024,512]{1,0:T(8,128)}, f32[1024,512]{1,0:T(8,128)}, u32[]{:S(2)}, u32[]{:S(2)}) collective-permute-start(f32[1024,512]{1,0:T(8,128)} %param.3), channel_id=1, source_target_pairs={{0,8},{8,0},{16,24},{24,16},{32,40},{40,32},{48,56},{56,48},{64,72... | collective-permute-start | bytes 6291464 | tf_op jit(solution)/shard_map/ppermute | solution.py:353
  84.8 9.2 %collective-permute-start.1 = (f32[128,256]{1,0:T(8,128)S(1)}, f32[128,256]{1,0:T(8,128)S(1)}, u32[]{:S(2)}, u32[]{:S(2)}) collective-permute-start(f32[128,256]{1,0:T(8,128)S(1)} %constant_dynamic-slice_fusion), channel_id=1, source_target_pairs={{0,0},{120,120},{8,16},{24,32},{40,48},{56,64},{72,80},{88,96},{10... | collective-permute-start | bytes 393224 | tf_op jit(solution)/shard_map/ppermute | solution.py:365
  88.4 3.1 %copy-start = (f32[3584,512]{1,0:T(8,128)S(1)}, f32[3584,512]{1,0:T(8,128)}, u32[]{:S(2)}) copy-start(f32[3584,512]{1,0:T(8,128)} %x_ref.7) | copy-start | bytes 22020100
  94.0 40.1 %collective-permute-start.7 = (f32[1024,256]{1,0:T(8,128)S(1)}, f32[1024,256]{1,0:T(8,128)S(1)}, u32[]{:S(2)}, u32[]{:S(2)}) collective-permute-start(f32[1024,256]{1,0:T(8,128)S(1)} %get-tuple-element.41), channel_id=1, source_target_pairs={{0,0},{120,120},{8,16},{24,32},{40,48},{56,64},{72,80},{88,96},{10... | collective-permute-start | bytes 3145736 | tf_op jit(solution)/shard_map/ppermute | solution.py:353
  97.6 40.1 %collective-permute-start.10 = (f32[1024,256]{1,0:T(8,128)S(1)}, f32[1024,256]{1,0:T(8,128)S(1)}, u32[]{:S(2)}, u32[]{:S(2)}) collective-permute-start(f32[1024,256]{1,0:T(8,128)S(1)} %get-tuple-element.45), channel_id=1, source_target_pairs={{0,8},{8,0},{16,24},{24,16},{32,40},{40,32},{48,56},{56,48},{64,72... | collective-permute-start | bytes 3145736 | tf_op jit(solution)/shard_map/ppermute | solution.py:353
  100.8 55.8 %collective-permute-start.4 = (f32[1024,256]{1,0:T(8,128)S(1)}, f32[1024,256]{1,0:T(8,128)S(1)}, u32[]{:S(2)}, u32[]{:S(2)}) collective-permute-start(f32[1024,256]{1,0:T(8,128)S(1)} %get-tuple-element.37), channel_id=1, source_target_pairs={{0,0},{120,120},{8,16},{24,32},{40,48},{56,64},{72,80},{88,96},{10... | collective-permute-start | bytes 3145736 | tf_op jit(solution)/shard_map/ppermute | solution.py:353
  104.3 29.8 %collective-permute-start.11 = (f32[512,256]{1,0:T(8,128)S(1)}, f32[512,256]{1,0:T(8,128)S(1)}, u32[]{:S(2)}, u32[]{:S(2)}) collective-permute-start(f32[512,256]{1,0:T(8,128)S(1)} %get-tuple-element.27.t_inner), channel_id=1, source_target_pairs={{0,8},{8,0},{16,24},{24,16},{32,40},{40,32},{48,56},{56,48},{64,72... | collective-permute-start | bytes 1572872 | tf_op jit(solution)/shard_map/ppermute | solution.py:364
  106.6 67.0 %collective-permute-start.6 = (f32[1024,256]{1,0:T(8,128)S(1)}, f32[1024,256]{1,0:T(8,128)S(1)}, u32[]{:S(2)}, u32[]{:S(2)}) collective-permute-start(f32[1024,256]{1,0:T(8,128)S(1)} %get-tuple-element.39), channel_id=1, source_target_pairs={{0,8},{8,0},{16,24},{24,16},{32,40},{40,32},{48,56},{56,48},{64,72... | collective-permute-start | bytes 3145736 | tf_op jit(solution)/shard_map/ppermute | solution.py:353
  134.1 38.1 %collective-permute-start.9 = (f32[1024,256]{1,0:T(8,128)S(1)}, f32[1024,256]{1,0:T(8,128)S(1)}, u32[]{:S(2)}, u32[]{:S(2)}) collective-permute-start(f32[1024,256]{1,0:T(8,128)S(1)} %get-tuple-element.43), channel_id=1, source_target_pairs={{0,8},{8,0},{16,24},{24,16},{32,40},{40,32},{48,56},{56,48},{64,72... | collective-permute-start | bytes 3145736 | tf_op jit(solution)/shard_map/ppermute | solution.py:353
  134.1 39.5 %collective-permute-start.8 = (f32[1024,256]{1,0:T(8,128)S(1)}, f32[1024,256]{1,0:T(8,128)S(1)}, u32[]{:S(2)}, u32[]{:S(2)}) collective-permute-start(f32[1024,256]{1,0:T(8,128)S(1)} %get-tuple-element.42), channel_id=1, source_target_pairs={{0,0},{120,120},{8,16},{24,32},{40,48},{56,64},{72,80},{88,96},{10... | collective-permute-start | bytes 3145736 | tf_op jit(solution)/shard_map/ppermute | solution.py:353
  137.7 4.9 %collective-permute-start.14 = (f32[128,256]{1,0:T(8,128)S(1)}, f32[128,256]{1,0:T(8,128)S(1)}, u32[]{:S(2)}, u32[]{:S(2)}) collective-permute-start(f32[128,256]{1,0:T(8,128)S(1)} %collective-permute-done.1.rest_0_), channel_id=1, source_target_pairs={{0,6},{1,7},{2,0},{3,1},{4,2},{5,3},{6,4},{7,5},{8,14},{9,15},{10,... | collective-permute-start | bytes 393224 | tf_op jit(solution)/shard_map/ppermute | solution.py:377
  142.6 15.1 %collective-permute-start.13 = (f32[128,256]{1,0:T(8,128)S(1)}, f32[128,256]{1,0:T(8,128)S(1)}, u32[]{:S(2)}, u32[]{:S(2)}) collective-permute-start(f32[128,256]{1,0:T(8,128)S(1)} %collective-permute-done.1.rest_0_), channel_id=1, source_target_pairs={{0,4},{1,5},{2,6},{3,7},{4,0},{5,1},{6,2},{7,3},{8,12},{9,13},{10,... | collective-permute-start | bytes 393224 | tf_op jit(solution)/shard_map/ppermute | solution.py:377
  156.6 5.0 %collective-permute-start.12 = (f32[128,256]{1,0:T(8,128)S(1)}, f32[128,256]{1,0:T(8,128)S(1)}, u32[]{:S(2)}, u32[]{:S(2)}) collective-permute-start(f32[128,256]{1,0:T(8,128)S(1)} %collective-permute-done.1.rest_0_), channel_id=1, source_target_pairs={{0,2},{1,3},{2,4},{3,5},{4,6},{5,7},{6,0},{7,1},{8,10},{9,11},{10,... | collective-permute-start | bytes 393224 | tf_op jit(solution)/shard_map/ppermute | solution.py:377
  157.7 17.4 %collective-permute-start = (f32[512,256]{1,0:T(8,128)S(1)}, f32[512,256]{1,0:T(8,128)S(1)}, u32[]{:S(2)}, u32[]{:S(2)}) collective-permute-start(f32[512,256]{1,0:T(8,128)S(1)} %get-tuple-element.29), channel_id=1, source_target_pairs={{0,8},{8,0},{16,24},{24,16},{32,40},{40,32},{48,56},{56,48},{64,72... | collective-permute-start | bytes 1572872 | tf_op jit(solution)/shard_map/ppermute | solution.py:353
  161.6 17.4 %collective-permute-start.5 = (f32[512,256]{1,0:T(8,128)S(1)}, f32[512,256]{1,0:T(8,128)S(1)}, u32[]{:S(2)}, u32[]{:S(2)}) collective-permute-start(f32[512,256]{1,0:T(8,128)S(1)} %get-tuple-element.38), channel_id=1, source_target_pairs={{0,0},{120,120},{8,16},{24,32},{40,48},{56,64},{72,80},{88,96},{10... | collective-permute-start | bytes 1572872 | tf_op jit(solution)/shard_map/ppermute | solution.py:353
